TPU v7x, 128 devices: a whole 4x4x4 slice. The times are simulated.
128 devices in a mesh: tm: 2 (over y_hi), lat: 4 (over x), lon: 16 (over y_lo, z, core).
Axes of the slice: x: 4, y: 4 (y_hi: 2, y_lo: 2; y = y_hi * 2 + y_lo), z: 4, core: 2. Of those that a mesh axis runs over, the one named last changes fastest.
Arguments:
- latents: bfloat16 [4, 160, 512, 384], P('tm', 'lat', 'lon'), may hold values from -60 to 60
- conv_weight: bfloat16 [3, 3, 3, 384, 384], replicated, may hold values from -0.0625 to 0.0625
- conv_bias: float32 [384], replicated, may hold values from -4 to 4
- norm_gain: float32 [384], replicated, may hold values from 0.5 to 1.5
- norm_shift: float32 [384], replicated, may hold values from -3 to 3
Outputs:
- decoded: bfloat16 [4, 160, 512, 384], P('tm', 'lat', 'lon')
All inputs are finite; a program needn't handle non-finite values.
Results may differ from a plain program's by a relative error of at most 0.00065.
Values may be sent and summed in bfloat16 or wider, within the bound.
A program may use at most 192 MiB of HBM per device.

v0:
```python
import jax
import jax.numpy as jnp
from jax import lax
from jax.sharding import PartitionSpec as P

GROUPS = 32


def with_halo(array, sides, width, wrap):
    for axis, dim in sides:
        peers, length = (lax.axis_size(axis), array.shape[dim])
        up = [(i, (i + 1) % peers) for i in range(peers if wrap else peers - 1)]
        down = [(j, i) for i, j in up]
        last = lax.slice_in_dim(array, length - width, length, axis=dim)
        initial = lax.slice_in_dim(array, 0, width, axis=dim)
        before = lax.ppermute(last, axis, up)
        after = lax.ppermute(initial, axis, down)
        array = jnp.concatenate([before, array, after], axis=dim)
    return array


def from_behind(block, axis, distance):
    devices = range(lax.axis_size(axis))
    route = [(i - distance, i) for i in devices if i - distance in devices]
    return lax.ppermute(block, axis, route)


def add_rims(frame_stack):
    lat_ext = with_halo(frame_stack, (("lat", 1),), 1, False)
    return with_halo(lat_ext, (("lon", 2),), 1, True)


def body(latents, conv_weight, conv_bias, norm_gain, norm_shift):
    frame_count, lat_cells, lon_cells, channels = latents.shape
    cached = from_behind(latents, "tm", 1)
    rimmed = add_rims(jnp.concatenate([cached, latents], axis=0))
    row_total = frame_count * lat_cells * lon_cells
    conv_out = jnp.zeros((row_total, channels), jnp.float32)
    for depth_a in range(3):
        for row_b in range(3):
            row_band = rimmed[depth_a : depth_a + frame_count, row_b : row_b + lat_cells]
            stacked = jnp.concatenate(
                [row_band[:, :, col_k : col_k + lon_cells] for col_k in range(3)], axis=3
            )
            stacked = stacked.reshape(row_total, 3 * channels)
            kernel = conv_weight[depth_a, row_b].reshape(3 * channels, channels)
            conv_out = conv_out + jnp.dot(stacked, kernel, preferred_element_type=jnp.float32)
    conv_out = conv_out + conv_bias[None, :]
    grouped = conv_out.reshape(row_total, GROUPS, channels // GROUPS)
    cell_count = (
        row_total
        * lax.axis_size("tm")
        * lax.axis_size("lat")
        * lax.axis_size("lon")
        * (channels // GROUPS)
    )
    local_sum = jnp.sum(grouped, axis=(0, 2))
    group_mean = lax.psum(local_sum, ("tm", "lat", "lon")) / cell_count
    centered = grouped - group_mean[None, :, None]
    group_var = (
        lax.psum(jnp.sum(centered * centered, axis=(0, 2)), ("tm", "lat", "lon")) / cell_count
    )
    inv_std = lax.rsqrt(group_var + 1e-06)
    normed = (centered * inv_std[None, :, None]).reshape(
        row_total, channels
    ) * norm_gain + norm_shift
    decoded = jax.nn.silu(normed).astype(jnp.bfloat16)
    return decoded.reshape(frame_count, lat_cells, lon_cells, channels)


def solution(mesh):
    return jax.shard_map(
        body,
        mesh=mesh,
        in_specs=(P("tm", "lat", "lon", None), P(), P(), P(), P()),
        out_specs=P("tm", "lat", "lon", None),
        check_vma=False,
    )
```

profile of v0, /device:TPU:16, one launch (start us, length us, event | category | flops | bytes accessed | tf_op | source)
XLA Modules:
  0.0 305.0 jit_solution(17867247665421024771)
XLA Ops:
  0.0 1.5 collective-permute-start
  1.6 46.9 %collective-permute-done = bf16[2,40,32,384]{3,2,1,0:T(8,128)(2,1)S(1)} collective-permute-done((bf16[2,40,32,384]{3,2,1,0:T(8,128)(2,1)}, bf16[2,40,32,384]{3,2,1,0:T(8,128)(2,1)S(1)}, u32[]{:S(2)}, u32[]{:S(2)}) %collective-permute-start) | collective-permute-done | bytes 1966112 | tf_op jit(solution)/shard_map/ppermute | solution.py:25
  48.6 2.5 constant_dynamic-update-slice_fusion
  51.1 3.4 %collective-permute-start.1 = (bf16[4,1,32,384]{3,2,1,0:T(8,128)(2,1)S(1)}, bf16[4,1,32,384]{3,2,1,0:T(8,128)(2,1)S(1)}, u32[]{:S(2)}, u32[]{:S(2)}) collective-permute-start(bf16[4,1,32,384]{3,2,1,0:T(8,128)(2,1)S(1)} %get-tuple-element.45), channel_id=1, source_target_pairs={{0,16},{16,32},{32,48},{1,17},{17,33},{33,49},{2,18},{18,34},{34,5... | collective-permute-start | bytes 294920 | tf_op jit(solution)/shard_map/ppermute | solution.py:16
  54.5 1.3 collective-permute-start.2
  55.8 3.5 %fusion.10 = (bf16[1,1,3,384,384]{4,3,2,1,0:T(8,128)(2,1)S(1)}, bf16[1,1,3,384,384]{4,3,2,1,0:T(8,128)(2,1)}, bf16[1,1,3,384,384]{4,3,2,1,0:T(8,128)(2,1)}, bf16...) fusion(bf16[3,3,3,384,384]{4,3,2,1,0:T(8,128)(2,1)S(1)} %copy-done), kind=kLoop, calls=%fused_computation.44 | loop fusion | bytes 15925248 | tf_op jit(solution)/shard_map/slice | solution.py:46
  59.4 1.7 collective-permute-done.2
  61.6 4.2 %collective-permute-start.4 = (bf16[4,42,1,384]{3,1,2,0:T(8,128)(2,1)S(1)}, bf16[4,42,1,384]{3,1,2,0:T(8,128)(2,1)S(1)}, u32[]{:S(2)}, u32[]{:S(2)}) collective-permute-start(bf16[4,42,1,384]{3,1,2,0:T(8,128)(2,1)S(1)} %copy.11), channel_id=1, source_target_pairs={{1,0},{2,1},{3,2},{4,3},{5,4},{6,5},{7,6},{8,7},{9,8},{10,9},{11,1... | collective-permute-start | bytes 387080 | tf_op jit(solution)/shard_map/ppermute | solution.py:17
  65.8 3.9 %fusion.6 = (bf16[2,40,32,384]{3,2,1,0:T(8,128)(2,1)}, bf16[2,40,32,384]{3,2,1,0:T(8,128)(2,1)}, bf16[2,40,32,384]{3,2,1,0:T(8,128)(2,1)}, bf16[2,40,32,384]{3,2,1,0:T(8,128)(2,1)}, bf16[2,40,32,384]{3,2,1,0:T(8,128)(2,1)}) fusion(bf16[4,40,32,384]{3,2,1,0:T(8,128)(2,1)S(1)} %constant_dynamic-update-slice_fusion, ...), kind=kLoop, calls=%fused_computation.33 | loop fusion | flops 3932160 | bytes 15925248 | tf_op jit(solution)/shard_map/concatenate | solution.py:18
  70.2 6.0 %maximum_maximum_fusion = (bf16[4,42,33,384]{3,2,1,0:T(8,128)(2,1)}, bf16[4,42,33,384]{3,2,1,0:T(8,128)(2,1)}) fusion(bf16[4,1,32,384]{3,2,1,0:T(8,128)(2,1)S(1)} %collective-permute-done.2, bf16[4,40,32,384]{3,2,1,0:T(8,128)(2,1)S(1)} %constant_dynamic-update-slice_fusion, bf16[4,1,32,384]{3,2,1,0:T(8,128)(2,1)S(1)} %collective-permute-done.1, ...), kind=kLoop, calls=%fused_computation.17 | loop fusion | flops 34062336 | bytes 12902400 | tf_op jit(solution)/shard_map/concatenate | solution.py:18
  76.2 26.5 %fusion.11 = (bf16[2,40,32,384]{3,2,1,0:T(8,128)(2,1)}, bf16[2,40,32,384]{3,2,1,0:T(8,128)(2,1)}, bf16[2,40,32,384]{3,2,1,0:T(8,128)(2,1)}, bf16[2,40,32,384]{3,...) fusion(bf16[4,42,33,384]{3,2,1,0:T(8,128)(2,1)} %get-tuple-elem, ...), kind=kLoop, calls=%fused_computation.45 | loop fusion | bytes 70778880 | tf_op jit(solution)/shard_map/slice | solution.py:43
  102.7 3.6 %pad_maximum_fusion.3 = bf16[2,40,32,1152]{3,2,1,0:T(8,128)(2,1)S(1)} fusion(bf16[2,40,32,384]{3,2,1,0:T(8,128)(2,1)} %get-tuple-element.50, bf16[2,40,32,384]{3,2,1,0:T(8,128)(2,1)} %copy-done.2, bf16[2,40,32,384]{3,2,1,0:T(8,128)(2,1)} %get-tuple-element.21), kind=kLoop, calls=%fused_computation.7 | loop fusion | flops 17694720 | bytes 11796480 | tf_op jit(solution)/shard_map/concatenate | solution.py:42
  106.4 5.4 %fusion.16 = f32[2560,384]{1,0:T(8,128)} fusion(bf16[2560,1152]{1,0:T(8,128)(2,1)S(1)} %bitcast.43, bf16[1152,384]{1,0:T(8,128)(2,1)S(1)} %bitcast.54), kind=kOutput, calls=%fused_computation.50 | convolution fusion | flops 2264924160 | bytes 10715136 | tf_op jit(solution)/shard_map/dot_general | solution.py:47
  111.8 1.5 pad_maximum_fusion.2
  113.3 5.3 %fusion.15 = f32[2560,384]{1,0:T(8,128)} fusion(bf16[2560,1152]{1,0:T(8,128)(2,1)S(1)} %bitcast.44, bf16[1152,384]{1,0:T(8,128)(2,1)S(1)} %bitcast.53), kind=kOutput, calls=%fused_computation.49 | convolution fusion | flops 2264924160 | bytes 10715136 | tf_op jit(solution)/shard_map/dot_general | solution.py:47
  118.6 0.9 pad_maximum_fusion.8
  119.8 5.3 %fusion.17 = f32[2560,384]{1,0:T(8,128)} fusion(bf16[2560,1152]{1,0:T(8,128)(2,1)S(1)} %bitcast.45, bf16[1152,384]{1,0:T(8,128)(2,1)S(1)} %bitcast.52), kind=kOutput, calls=%fused_computation.51 | convolution fusion | flops 2264924160 | bytes 10715136 | tf_op jit(solution)/shard_map/dot_general | solution.py:47
  125.1 0.9 pad_maximum_fusion.7
  127.8 0.9 pad_maximum_fusion.6
  130.5 0.9 pad_maximum_fusion.5
  133.3 5.0 %pad_maximum_fusion.4 = bf16[2,40,32,1152]{3,2,1,0:T(8,128)(2,1)} fusion(bf16[2,40,32,384]{3,2,1,0:T(8,128)(2,1)S(1)} %copy-done.13, bf16[2,40,32,384]{3,2,1,0:T(8,128)(2,1)S(1)} %copy-done.3, bf16[2,40,32,384]{3,2,1,0:T(8,128)(2,1)S(1)} %copy-done.12), kind=kLoop, calls=%fused_computation.8 | loop fusion | flops 17694720 | bytes 11796480 | tf_op jit(solution)/shard_map/concatenate | solution.py:42
  138.3 7.6 %convolution_add_fusion.5 = f32[2560,384]{1,0:T(8,128)S(1)} fusion(bf16[2560,1152]{1,0:T(8,128)(2,1)} %bitcast.42, bf16[1152,384]{1,0:T(8,128)(2,1)S(1)} %bitcast.51, f32[2560,384]{1,0:T(8,128)} %fusion.15, f32[2560,384]{1,0:T(8,128)S(1)} %copy-done.36), kind=kOutput, calls=%fused_computation.26 | convolution fusion | flops 2266890240 | bytes 18579456 | tf_op jit(solution)/shard_map/dot_general | solution.py:47
  146.0 3.4 %convolution_add_fusion.4 = f32[2560,384]{1,0:T(8,128)S(1)} fusion(f32[2560,384]{1,0:T(8,128)S(1)} %convolution_add_fusion.5, bf16[2560,1152]{1,0:T(8,128)(2,1)S(1)} %bitcast.40, bf16[1152,384]{1,0:T(8,128)(2,1)S(1)} %bitcast.50), kind=kOutput, calls=%fused_computation.25 | convolution fusion | flops 2265907200 | bytes 14647296 | tf_op jit(solution)/shard_map/dot_general | solution.py:47
  149.4 3.4 %convolution_add_fusion.3 = f32[2560,384]{1,0:T(8,128)S(1)} fusion(f32[2560,384]{1,0:T(8,128)S(1)} %convolution_add_fusion.4, bf16[2560,1152]{1,0:T(8,128)(2,1)S(1)} %bitcast.38, bf16[1152,384]{1,0:T(8,128)(2,1)S(1)} %bitcast.49), kind=kOutput, calls=%fused_computation.24 | convolution fusion | flops 2265907200 | bytes 14647296 | tf_op jit(solution)/shard_map/dot_general | solution.py:47
  152.9 3.7 %convolution_add_fusion.2 = f32[2560,384]{1,0:T(8,128)S(1)} fusion(f32[2560,384]{1,0:T(8,128)S(1)} %convolution_add_fusion.3, bf16[2560,1152]{1,0:T(8,128)(2,1)S(1)} %bitcast.37, bf16[1152,384]{1,0:T(8,128)(2,1)S(1)} %bitcast.48), kind=kOutput, calls=%fused_computation.23 | convolution fusion | flops 2265907200 | bytes 14647296 | tf_op jit(solution)/shard_map/dot_general | solution.py:47
  156.6 2.7 fusion.1
  159.4 3.5 %fusion.5 = f32[2560,384]{1,0:T(8,128)S(1)} fusion(f32[2560,384]{1,0:T(8,128)S(1)} %copy-done.35, f32[2560,384]{1,0:T(8,128)S(1)} %convolution_add_fusion.2, bf16[2560,1152]{1,0:T(8,128)(2,1)S(1)} %bitcast.41, bf16[1152,384]{1,0:T(8,128)(2,1)S(1)} %bitcast.47), kind=kOutput, calls=%fused_computation.22 | convolution fusion | flops 2266890240 | bytes 18579456 | tf_op jit(solution)/shard_map/dot_general | solution.py:47
  162.8 5.6 %fusion.14 = (f32[384]{0:T(512)S(1)}, f32[2560,384]{1,0:T(8,128)}) fusion(f32[384]{0:T(512)S(1)} %copy-done.34, f32[2560,384]{1,0:T(8,128)S(1)} %fusion.5, bf16[2560,1152]{1,0:T(8,128)(2,1)S(1)} %bitcast.39, bf16[1152,384]{1,0:T(8,128)(2,1)S(1)} %bitcast.46), kind=kOutput, calls=%fused_computation.48 | convolution fusion | flops 2267872768 | bytes 14650368 | tf_op jit(solution)/shard_map/dot_general | solution.py:47
  168.6 64.1 %psum.14 = f32[32]{0:T(128)S(1)} all-reduce(f32[32]{0:T(128)S(1)} %reduce_sum.25), channel_id=1, replica_groups=mesh['tm'=2,'lat'=4,'lon'=16] {'tm','lat','lon'}, use_global_device_ids=true, to_apply=%region_2.0 | all-reduce | flops 32 | bytes 256 | tf_op jit(solution)/shard_map/psum | solution.py:58
  233.0 2.6 multiply_reduce_fusion
  235.8 64.1 %psum.15 = f32[32]{0:T(128)S(1)} all-reduce(f32[32]{0:T(128)S(1)} %reduce_sum.37), channel_id=1, replica_groups=mesh['tm'=2,'lat'=4,'lon'=16] {'tm','lat','lon'}, use_global_device_ids=true, to_apply=%region_5.6 | all-reduce | flops 32 | bytes 256 | tf_op jit(solution)/shard_map/psum | solution.py:61
  300.1 4.6 %multiply_convert_fusion = bf16[2560,384]{1,0:T(8,128)(2,1)} fusion(f32[2560,384]{1,0:T(8,128)} %get-tuple-element.48, f32[384]{0:T(512)S(1)} %copy-done.32, f32[384]{0:T(512)S(1)} %copy-done.33, f32[384]{0:T(512)S(1)} %mul.31, f32[384]{0:T(512)S(1)} %sub.15), kind=kLoop, calls=%fused_computation.27 | loop fusion | flops 8847360 | bytes 5904384 | tf_op jit(solution)/shard_map/convert_element_type | solution.py:67
  (95 shorter events, 7.9 us)
Async XLA Ops:
  0.0 55.8 %copy-start = (bf16[3,3,3,384,384]{4,3,2,1,0:T(8,128)(2,1)S(1)}, bf16[3,3,3,384,384]{4,3,2,1,0:T(8,128)(2,1)}, u32[]{:S(2)}) copy-start(bf16[3,3,3,384,384]{4,3,2,1,0:T(8,128)(2,1)} %param.6) | copy-start | bytes 23887876
  0.0 48.4 %collective-permute-start = (bf16[2,40,32,384]{3,2,1,0:T(8,128)(2,1)}, bf16[2,40,32,384]{3,2,1,0:T(8,128)(2,1)S(1)}, u32[]{:S(2)}, u32[]{:S(2)}) collective-permute-start(bf16[2,40,32,384]{3,2,1,0:T(8,128)(2,1)} %param.5), channel_id=1, source_target_pairs={{0,64},{1,65},{2,66},{3,67},{4,68},{5,69},{6,70},{7,71},{8,72},{9,... | collective-permute-start | bytes 5898248 | tf_op jit(solution)/shard_map/ppermute | solution.py:25
  51.1 8.3 %collective-permute-start.1 = (bf16[4,1,32,384]{3,2,1,0:T(8,128)(2,1)S(1)}, bf16[4,1,32,384]{3,2,1,0:T(8,128)(2,1)S(1)}, u32[]{:S(2)}, u32[]{:S(2)}) collective-permute-start(bf16[4,1,32,384]{3,2,1,0:T(8,128)(2,1)S(1)} %get-tuple-element.45), channel_id=1, source_target_pairs={{0,16},{16,32},{32,48},{1,17},{17,33},{33,49},{2,18},{18,34},{34,5... | collective-permute-start | bytes 294920 | tf_op jit(solution)/shard_map/ppermute | solution.py:16
  54.5 6.5 %collective-permute-start.2 = (bf16[4,1,32,384]{3,2,1,0:T(8,128)(2,1)S(1)}, bf16[4,1,32,384]{3,2,1,0:T(8,128)(2,1)S(1)}, u32[]{:S(2)}, u32[]{:S(2)}) collective-permute-start(bf16[4,1,32,384]{3,2,1,0:T(8,128)(2,1)S(1)} %get-tuple-element.46), channel_id=1, source_target_pairs={{16,0},{32,16},{48,32},{17,1},{33,17},{49,33},{18,2},{34,18},{50,3... | collective-permute-start | bytes 294920 | tf_op jit(solution)/shard_map/ppermute | solution.py:17
  61.5 8.3 %collective-permute-start.3 = (bf16[4,42,1,384]{3,1,2,0:T(8,128)(2,1)S(1)}, bf16[4,42,1,384]{3,1,2,0:T(8,128)(2,1)S(1)}, u32[]{:S(2)}, u32[]{:S(2)}) collective-permute-start(bf16[4,42,1,384]{3,1,2,0:T(8,128)(2,1)S(1)} %copy.9), channel_id=1, source_target_pairs={{0,1},{1,2},{2,3},{3,4},{4,5},{5,6},{6,7},{7,8},{8,9},{9,10},{10,1... | collective-permute-start | bytes 387080 | tf_op jit(solution)/shard_map/ppermute | solution.py:16
  61.6 8.4 %collective-permute-start.4 = (bf16[4,42,1,384]{3,1,2,0:T(8,128)(2,1)S(1)}, bf16[4,42,1,384]{3,1,2,0:T(8,128)(2,1)S(1)}, u32[]{:S(2)}, u32[]{:S(2)}) collective-permute-start(bf16[4,42,1,384]{3,1,2,0:T(8,128)(2,1)S(1)} %copy.11), channel_id=1, source_target_pairs={{1,0},{2,1},{3,2},{4,3},{5,4},{6,5},{7,6},{8,7},{9,8},{10,9},{11,1... | collective-permute-start | bytes 387080 | tf_op jit(solution)/shard_map/ppermute | solution.py:17
  102.7 3.6 %copy-start.31 = (bf16[1,1,3,384,384]{4,3,2,1,0:T(8,128)(2,1)S(1)}, bf16[1,1,3,384,384]{4,3,2,1,0:T(8,128)(2,1)}, u32[]{:S(2)}) copy-start(bf16[1,1,3,384,384]{4,3,2,1,0:T(8,128)(2,1)} %get-tuple-element.11) | copy-start | bytes 2654212
  106.4 5.4 %copy-start.11 = (bf16[2,40,32,384]{3,2,1,0:T(8,128)(2,1)S(1)}, bf16[2,40,32,384]{3,2,1,0:T(8,128)(2,1)}, u32[]{:S(2)}) copy-start(bf16[2,40,32,384]{3,2,1,0:T(8,128)(2,1)} %get-tuple-element.43) | copy-start | bytes 5898244
  106.4 5.4 %copy-start.22 = (bf16[2,40,32,384]{3,2,1,0:T(8,128)(2,1)S(1)}, bf16[2,40,32,384]{3,2,1,0:T(8,128)(2,1)}, u32[]{:S(2)}) copy-start(bf16[2,40,32,384]{3,2,1,0:T(8,128)(2,1)} %get-tuple-element.22) | copy-start | bytes 5898244
  106.4 5.4 %copy-start.23 = (bf16[2,40,32,384]{3,2,1,0:T(8,128)(2,1)S(1)}, bf16[2,40,32,384]{3,2,1,0:T(8,128)(2,1)}, u32[]{:S(2)}) copy-start(bf16[2,40,32,384]{3,2,1,0:T(8,128)(2,1)} %get-tuple-element.49) | copy-start | bytes 5898244
  113.3 5.3 %copy-start.1 = (bf16[2,40,32,384]{3,2,1,0:T(8,128)(2,1)S(1)}, bf16[2,40,32,384]{3,2,1,0:T(8,128)(2,1)}, u32[]{:S(2)}) copy-start(bf16[2,40,32,384]{3,2,1,0:T(8,128)(2,1)} %param.5) | copy-start | bytes 5898244
  113.3 5.3 %copy-start.20 = (bf16[2,40,32,384]{3,2,1,0:T(8,128)(2,1)S(1)}, bf16[2,40,32,384]{3,2,1,0:T(8,128)(2,1)}, u32[]{:S(2)}) copy-start(bf16[2,40,32,384]{3,2,1,0:T(8,128)(2,1)} %get-tuple-element.15) | copy-start | bytes 5898244
  113.3 5.3 %copy-start.21 = (bf16[2,40,32,384]{3,2,1,0:T(8,128)(2,1)S(1)}, bf16[2,40,32,384]{3,2,1,0:T(8,128)(2,1)}, u32[]{:S(2)}) copy-start(bf16[2,40,32,384]{3,2,1,0:T(8,128)(2,1)} %get-tuple-element.56) | copy-start | bytes 5898244
  119.7 5.3 %copy-start.10 = (bf16[2,40,32,384]{3,2,1,0:T(8,128)(2,1)S(1)}, bf16[2,40,32,384]{3,2,1,0:T(8,128)(2,1)}, u32[]{:S(2)}) copy-start(bf16[2,40,32,384]{3,2,1,0:T(8,128)(2,1)} %get-tuple-element.36) | copy-start | bytes 5898244
  119.7 5.3 %copy-start.18 = (bf16[2,40,32,384]{3,2,1,0:T(8,128)(2,1)S(1)}, bf16[2,40,32,384]{3,2,1,0:T(8,128)(2,1)}, u32[]{:S(2)}) copy-start(bf16[2,40,32,384]{3,2,1,0:T(8,128)(2,1)} %get-tuple-element.17) | copy-start | bytes 5898244
  119.8 5.3 %copy-start.19 = (bf16[2,40,32,384]{3,2,1,0:T(8,128)(2,1)S(1)}, bf16[2,40,32,384]{3,2,1,0:T(8,128)(2,1)}, u32[]{:S(2)}) copy-start(bf16[2,40,32,384]{3,2,1,0:T(8,128)(2,1)} %get-tuple-element.54) | copy-start | bytes 5898244
  127.8 2.7 copy-start.15
  130.5 2.7 copy-start.13
  133.3 5.0 %copy-start.28 = (bf16[1,1,3,384,384]{4,3,2,1,0:T(8,128)(2,1)S(1)}, bf16[1,1,3,384,384]{4,3,2,1,0:T(8,128)(2,1)}, u32[]{:S(2)}) copy-start(bf16[1,1,3,384,384]{4,3,2,1,0:T(8,128)(2,1)} %get-tuple-element.10) | copy-start | bytes 2654212
  133.3 5.0 %copy-start.36 = (f32[2560,384]{1,0:T(8,128)S(1)}, f32[2560,384]{1,0:T(8,128)}, u32[]{:S(2)}) copy-start(f32[2560,384]{1,0:T(8,128)} %fusion.16) | copy-start | bytes 11796484
  138.3 7.6 %copy-start.27 = (bf16[1,1,3,384,384]{4,3,2,1,0:T(8,128)(2,1)S(1)}, bf16[1,1,3,384,384]{4,3,2,1,0:T(8,128)(2,1)}, u32[]{:S(2)}) copy-start(bf16[1,1,3,384,384]{4,3,2,1,0:T(8,128)(2,1)} %get-tuple-element.9) | copy-start | bytes 2654212
  145.9 3.4 %copy-start.26 = (bf16[1,1,3,384,384]{4,3,2,1,0:T(8,128)(2,1)S(1)}, bf16[1,1,3,384,384]{4,3,2,1,0:T(8,128)(2,1)}, u32[]{:S(2)}) copy-start(bf16[1,1,3,384,384]{4,3,2,1,0:T(8,128)(2,1)} %get-tuple-element.8) | copy-start | bytes 2654212
  149.4 3.4 %copy-start.25 = (bf16[1,1,3,384,384]{4,3,2,1,0:T(8,128)(2,1)S(1)}, bf16[1,1,3,384,384]{4,3,2,1,0:T(8,128)(2,1)}, u32[]{:S(2)}) copy-start(bf16[1,1,3,384,384]{4,3,2,1,0:T(8,128)(2,1)} %get-tuple-element.7) | copy-start | bytes 2654212
  152.8 3.7 %copy-start.6 = (bf16[2,40,32,384]{3,2,1,0:T(8,128)(2,1)S(1)}, bf16[2,40,32,384]{3,2,1,0:T(8,128)(2,1)}, u32[]{:S(2)}) copy-start(bf16[2,40,32,384]{3,2,1,0:T(8,128)(2,1)} %get-tuple-element.14) | copy-start | bytes 5898244
  152.8 3.7 %copy-start.7 = (bf16[2,40,32,384]{3,2,1,0:T(8,128)(2,1)S(1)}, bf16[2,40,32,384]{3,2,1,0:T(8,128)(2,1)}, u32[]{:S(2)}) copy-start(bf16[2,40,32,384]{3,2,1,0:T(8,128)(2,1)} %get-tuple-element.16) | copy-start | bytes 5898244
  152.9 3.7 %copy-start.8 = (bf16[2,40,32,384]{3,2,1,0:T(8,128)(2,1)S(1)}, bf16[2,40,32,384]{3,2,1,0:T(8,128)(2,1)}, u32[]{:S(2)}) copy-start(bf16[2,40,32,384]{3,2,1,0:T(8,128)(2,1)} %get-tuple-element.55) | copy-start | bytes 5898244
  152.9 3.7 %copy-start.9 = (bf16[2,40,32,384]{3,2,1,0:T(8,128)(2,1)S(1)}, bf16[2,40,32,384]{3,2,1,0:T(8,128)(2,1)}, u32[]{:S(2)}) copy-start(bf16[2,40,32,384]{3,2,1,0:T(8,128)(2,1)} %get-tuple-element.57) | copy-start | bytes 5898244
  156.6 2.8 copy-start.24
  156.6 2.8 copy-start.35
  159.4 3.5 %copy-start.34 = (f32[384]{0:T(512)S(1)}, f32[384]{0:T(512)}, u32[]{:S(2)}) copy-start(f32[384]{0:T(512)} %param.7) | copy-start | bytes 4612
  168.4 131.7 %copy-start.32 = (f32[384]{0:T(512)S(1)}, f32[384]{0:T(512)}, u32[]{:S(2)}) copy-start(f32[384]{0:T(512)} %param.9) | copy-start | bytes 4612
  168.4 131.7 %copy-start.33 = (f32[384]{0:T(512)S(1)}, f32[384]{0:T(512)}, u32[]{:S(2)}) copy-start(f32[384]{0:T(512)} %param.8) | copy-start | bytes 4612
  (10 other events, 19.1 us)
where the time goes:
time: 309 us; the launch traced here: 305 us
  blocking collectives  128 us (41%)
  waiting for transfers between devices  48.5 us (16%)
  matrix products  43.1 us (14%)
  local copies, waits for them, and re-layouts  39.7 us (13%)
  other arithmetic  34.1 us (11%)
  starting transfers between devices  10.5 us (3%)
    psum x1, blocking collectives, body(): group_mean = lax.psum(local_sum, ('tm', 'lat', 'lon')) / cell_count  64.1 us
    psum x1, blocking collectives, body(): lax.psum(jnp.sum(centered * centered, axis=(0, 2)), ('tm', 'lat', 'lon'))  64.1 us
    ppermute x1, waiting for transfers between devices, from_behind(): return lax.ppermute(block, axis, route)  46.9 us
    dot_general x9, matrix products, body(): jnp.dot(stacked, kernel, preferred_element_type=jnp.float32)  43.1 us
    slice x1, local copies, waits for them, and re-layouts, body(): row_band[:, :, col_k:col_k + lon_cells]  26.5 us
    concatenate x8, other arithmetic, body(): jnp.concatenate([row_band[:, :, col_k:col_k + lon_cells] for col_k in ran...  16.3 us
    concatenate x2, other arithmetic, with_halo(): array = jnp.concatenate([before, array, after], axis=dim)  9.93 us
  transfers between devices with their start and end apart: 5, of which 2 were waited for; matrix products, arithmetic and copies ran while one was open for 3% of the time, Pallas kernels for 0%

commit v1 on v0

v1 whole, which is shorter than its diff:
```python
import functools

import jax
import jax.numpy as jnp
from jax import lax
from jax.experimental import pallas as pl
from jax.experimental.pallas import tpu as pltpu
from jax.sharding import PartitionSpec as P

MESH = pl.DeviceIdType.MESH
F32, BF16 = jnp.float32, jnp.bfloat16
HIGH = lax.Precision.HIGHEST

GROUPS = 32
C = 384
PER = C // GROUPS
H, WD = 40, 32
N = 4
CHUNKS = H // N
EDGE = 16

SHARE_LO, SHARE_HI = 15, 29
BACK = (SHARE_HI - SHARE_LO + 2) // N
BACK_ROW = SHARE_LO - 1
OFF = 30
ACC_ROWS = 62


def chunk_row(c):
    odd = c % 2
    half = c // 2
    return N * ((1 - odd) * half + odd * (CHUNKS - 1 - half))


def kernel(
    x_ref, w_ref, bias_ref, gain_ref, shift_ref, o_ref,
    wt, xm, xl, xr, lh, rh, acc, out, g_in, g_out, aff, stat, r1, r2,
    loc_sem, w_sem, out_sem, main_s, main_r, strip_s, strip_r, row_s, row_r, r1_s, r1_r, r2_s, r2_r,
):
    tm, lat, lon = (lax.axis_index(a) for a in ("tm", "lat", "lon"))
    left, right = (lon + 15) % 16, (lon + 1) % 16
    z, yl = lon % 8, lon // 8
    first, second = tm == 0, tm == 1
    has_up, has_dn = lat > 0, lat < 3
    partner = (1 - tm, lat, lon)
    near = [(tm, lat, yl * 8 + (z + d) % 8) for d in range(1, 8)]
    far = [
        ((tm + a) % 2, (lat + b) % 4, ((yl + c) % 2) * 8 + z)
        for a in range(2) for b in range(4) for c in range(2)
    ][1:]
    corners = [(tm, (lat + b) % 4, l) for b in (0, 1, 3) for l in (left, right)]

    barrier = pltpu.get_barrier_semaphore()
    peers = far + near + corners
    for peer in peers:
        pl.semaphore_signal(barrier, inc=1, device_id=peer, device_id_type=MESH)

    def load_x(c):
        return pltpu.make_async_copy(
            x_ref.at[:, pl.ds(c * N, N)], xm.at[pl.ds(2, 2), pl.ds(c * N + 1, N)], loc_sem.at[c])

    def load_w(a):
        return pltpu.make_async_copy(w_ref.at[a], wt.at[a], w_sem.at[a])

    load_x(0).start()
    load_w(2).start()
    load_w(1).start()
    for c in range(1, CHUNKS):
        load_x(c).start()
    load_w(0).start()

    row_i = lax.broadcasted_iota(jnp.int32, (C, 128), 0)
    lane_i = lax.broadcasted_iota(jnp.int32, (C, 128), 1)
    delta = row_i - PER * lane_i
    g_in[...] = jnp.where((delta >= 0) & (delta < PER), 1.0, 0.0)
    row_i = lax.broadcasted_iota(jnp.int32, (128, C), 0)
    lane_i = lax.broadcasted_iota(jnp.int32, (128, C), 1)
    delta = lane_i - PER * row_i
    g_out[...] = jnp.where((delta >= 0) & (delta < PER), 1.0, 0.0)

    pl.semaphore_wait(barrier, len(peers))

    def remote(src, dst, s, r, dev):
        return pltpu.make_async_remote_copy(
            src_ref=src, dst_ref=dst, send_sem=s, recv_sem=r, device_id=dev, device_id_type=MESH)

    def main(c, row):
        return remote(
            x_ref.at[:, pl.ds(row, N)], xm.at[pl.ds(0, 2), pl.ds(row + 1, N)],
            main_s.at[c], main_r.at[c], partner)

    def strip(k, c, p, side):
        cols = pl.ds(WD - EDGE, EDGE) if side == 0 else pl.ds(0, EDGE)
        src = (
            x_ref.at[:, pl.ds(p - 1, N), cols] if k else xm.at[pl.ds(0, 2), pl.ds(p, N), cols])
        dst = (lh, rh)[side].at[pl.ds(2 * k, 2), pl.ds(p, N)]
        return remote(src, dst, strip_s.at[k, c, side], strip_r.at[k, c, side],
                      (tm, lat, (right, left)[side]))

    def rows(k, way):
        p = H if way == 0 else 1
        q = 0 if way == 0 else H + 1
        la = (lat + 1) % 4 if way == 0 else (lat + 3) % 4
        base = x_ref.at[:, pl.ds(p - 1, 1)] if k else xm.at[pl.ds(0, 2), pl.ds(p, 1)]
        to = (pl.ds(2 * k, 2), pl.ds(q, 1))
        ss, rs = row_s.at[k, way], row_r.at[k, way]
        return [
            remote(base, xm.at[to], ss.at[0], rs.at[0], (tm, la, lon)),
            remote(base.at[:, :, pl.ds(WD - EDGE, EDGE)], lh.at[to], ss.at[1], rs.at[1], (tm, la, right)),
            remote(base.at[:, :, pl.ds(0, EDGE)], rh.at[to], ss.at[2], rs.at[2], (tm, la, left)),
        ]

    def rows_start(k, way):
        @pl.when(has_dn if way == 0 else has_up)
        def _():
            for cp in rows(k, way):
                cp.start()

    for way in (0, 1):
        rows_start(1, way)
    for c in range(2):
        for side in (0, 1):
            strip(1, c, c * N + 1, side).start()

    @pl.when(first)
    def _():
        for c in range(CHUNKS):
            main(c, chunk_row(c)).start()

    @pl.when(second)
    def _():
        for c in range(BACK):
            main(c, BACK_ROW + c * N).start()

    for c in range(2, CHUNKS):
        for side in (0, 1):
            strip(1, c, c * N + 1, side).start()

    bias = jnp.broadcast_to(bias_ref[...][None], (2, WD, C))

    def fill(r, carry):
        acc[:, r] = bias
        return carry

    lax.fori_loop(0, ACC_ROWS, fill, 0)

    def shifted(slot, p):
        col = lax.broadcasted_iota(jnp.int32, (WD, C), 0)
        for f in range(2):
            v = xm[slot + f, p].astype(F32)
            a = lh[slot + f, p].astype(F32)[EDGE - 1:]
            b = rh[slot + f, p].astype(F32)[:1]
            xl[slot + f, p] = jnp.where(col == 0, a, pltpu.roll(v, 1, 0)).astype(BF16)
            xr[slot + f, p] = jnp.where(col == WD - 1, b, pltpu.roll(v, WD - 1, 0)).astype(BF16)

    def planes(slot, p, n, own, off, taps=(0, 1, 2)):
        m = n * WD
        both = jnp.concatenate(
            [v[pl.ds(slot, 2), pl.ds(p, n)].reshape(2 * m, C) for v in (xl, xm, xr)], axis=1)
        one = both[:m] if own else both[m:]
        same, target = (2, 1) if own else (0, 0)
        for b in taps:
            rr = pl.ds(p + 1 - b + off, n)
            y = jnp.dot(both, wt[same, b], preferred_element_type=F32)
            acc[:, rr] += y.reshape(2, n, WD, C)
            y = jnp.dot(one, wt[1, b], preferred_element_type=F32)
            acc[target, rr] += y.reshape(n, WD, C)

    def edges(k):
        for way in (0, 1):
            @pl.when(has_up if way == 0 else has_dn)
            def _():
                for cp in rows(k, way):
                    cp.wait_recv()
                p = 0 if way == 0 else H + 1
                shifted(2 * k, p)
                planes(2 * k, p, 1, k == 1, 0, (0,) if way == 0 else (2,))

    def other_p(c):
        return jnp.where(first, BACK_ROW + 1 + c * N, chunk_row(c) + 1)

    def arrive(c):
        p = other_p(c)
        main(c, p - 1).wait_recv()
        for side in (0, 1):
            strip(0, c, p, side).start()

        @pl.when(second & (c == 0))
        def _():
            rows_start(0, 1)

        @pl.when(second & (c == 1))
        def _():
            rows_start(0, 0)

    load_w(2).wait()
    load_w(1).wait()

    def own_step(i, carry):
        mine = i < CHUNKS
        j = jnp.maximum(i - CHUNKS, 0)
        slot = jnp.where(mine, 2, 0)
        p = jnp.where(mine, 1 + i * N, BACK_ROW + 1 + j * N)

        @pl.when(mine)
        def _():
            load_x(i).wait()
            for side in (0, 1):
                strip(1, i, p, side).wait_recv()

        @pl.when(first & (i >= CHUNKS - 1) & (i < CHUNKS - 1 + BACK))
        def _():
            arrive(i - (CHUNKS - 1))

        @pl.when(i >= CHUNKS)
        def _():
            for side in (0, 1):
                strip(0, j, p, side).wait_recv()

        for r in range(N):
            shifted(slot, p + r)
        planes(slot, p, N, True, jnp.where(mine, 0, OFF))
        return carry

    lax.fori_loop(0, jnp.where(first, CHUNKS + BACK, CHUNKS), own_step, 0)
    edges(1)
    load_w(0).wait()

    count = jnp.where(first, 54.0, 26.0) * (2 * WD * PER)
    other_count = jnp.where(first, 26.0, 54.0) * (2 * WD * PER)
    sub = lax.broadcasted_iota(jnp.int32, (8, 128), 0)

    def pack(mean, m2):
        return jnp.where(sub == 0, mean, jnp.where(sub == 1, m2, 0.0))

    def over_rows(f):
        def step(r, a):
            return a + f(acc[:, r].reshape(2 * WD // 8, 8, C)).sum(0)
        a = lax.fori_loop(1, jnp.where(first, 41, 1 + SHARE_LO), step, jnp.zeros((8, C), F32))
        a = lax.fori_loop(
            jnp.where(first, 1 + SHARE_LO + OFF, 1 + SHARE_HI), jnp.where(first, 1 + SHARE_HI + OFF, 41), step, a)
        return jnp.broadcast_to(a.sum(0, keepdims=True), (8, C))

    def group(v):
        return jnp.dot(v, g_in[...], precision=HIGH, preferred_element_type=F32)

    def channel(v):
        return jnp.dot(v, g_out[...], precision=HIGH, preferred_element_type=F32)

    def r1_copy(i):
        return remote(r1.at[0], r1.at[i + 1], r1_s.at[i], r1_r.at[i], near[i])

    def r2_copy(i):
        return remote(r2.at[0], r2.at[i + 1], r2_s.at[i], r2_r.at[i], far[i])

    def stats_begin():
        mean = group(over_rows(lambda v: v)) / count
        mean_c = channel(mean)
        m2 = group(over_rows(lambda v: (v - mean_c) * (v - mean_c)))
        r1[0] = pack(mean, m2)
        for i in range(7):
            r1_copy(i).start()

    def stats_middle():
        for i in range(7):
            r1_copy(i).wait_recv()
        means = [r1[i, 0:1] for i in range(8)]
        mean = sum(means) * 0.125
        m2 = sum(r1[i, 1:2] for i in range(8)) + count * sum((m - mean) * (m - mean) for m in means)
        r2[0] = pack(jnp.broadcast_to(mean, (8, 128)), jnp.broadcast_to(m2, (8, 128)))
        for i in range(15):
            r2_copy(i).start()

    def stats_end():
        for i in range(15):
            r2_copy(i).wait_recv()
        means = [r2[i, 0:1] for i in range(16)]
        mine, other = 8.0 * count, 8.0 * other_count
        total = 8.0 * (mine + other)
        mean = (mine * sum(means[:8]) + other * sum(means[8:])) / total
        m2 = sum(r2[i, 1:2] for i in range(16))
        m2 = m2 + mine * sum((m - mean) * (m - mean) for m in means[:8])
        m2 = m2 + other * sum((m - mean) * (m - mean) for m in means[8:])
        inv = lax.rsqrt(m2 / total + 1e-6)
        both = channel(pack(jnp.broadcast_to(mean, (8, 128)), jnp.broadcast_to(inv, (8, 128))))
        aff[0:1] = both[0:1]
        aff[1:2] = both[1:2] * gain_ref[...]

    def finish(lo, hi):
        mean, scale, shift = aff[0:1], aff[1:2], shift_ref[...]

        def step(r, carry):
            v = acc[:, r + 1].reshape(2 * WD, C)
            v = (v - mean) * scale + shift
            v = v / (1.0 + jnp.exp(-v))
            out[:, r] = v.astype(BF16).reshape(2, WD, C)
            return carry

        lax.fori_loop(lo, hi, step, 0)

    def store(lo, hi, i):
        return pltpu.make_async_copy(
            out.at[:, pl.ds(lo, hi - lo)], o_ref.at[:, pl.ds(lo, hi - lo)], out_sem.at[i])

    @pl.when(second)
    def _():
        arrive(0)

    last_whole = 7

    def prev_step(s, carry):
        @pl.when(second & (s < last_whole))
        def _():
            arrive(s)

        p = other_p(s - 1)
        slot = jnp.where(first, 2, 0)

        @pl.when(second)
        def _():
            for side in (0, 1):
                strip(0, s - 1, p, side).wait_recv()
            for r in range(N):
                shifted(0, p + r)

        planes(slot, p, N, False, jnp.where(first, OFF, 0))

        @pl.when(second & (s == 4))
        def _():
            edges(0)

        @pl.when(second & (s == last_whole))
        def _():
            stats_begin()

        @pl.when(second & (s == last_whole + 1))
        def _():
            stats_middle()

        @pl.when(second & (s >= last_whole) & (s < CHUNKS))
        def _():
            arrive(s)

        @pl.when(second & (s == last_whole + 2))
        def _():
            stats_end()
            finish(0, SHARE_LO)
            finish(SHARE_HI, H)
            store(0, SHARE_LO, 0).start()
            store(SHARE_HI, H, 1).start()

        return carry

    lax.fori_loop(1, jnp.where(first, BACK, CHUNKS) + 1, prev_step, 0)

    @pl.when(first)
    def _():
        stats_begin()
        stats_middle()
        stats_end()
        finish(0, SHARE_LO)
        finish(SHARE_HI, H)
        store(0, SHARE_LO, 0).start()
        store(SHARE_HI, H, 1).start()

    finish(SHARE_LO, SHARE_HI)
    store(SHARE_LO, SHARE_HI, 2).start()

    for i in range(7):
        r1_copy(i).wait_send()
    for i in range(15):
        r2_copy(i).wait_send()
    for c in range(CHUNKS):
        for side in (0, 1):
            strip(1, c, c * N + 1, side).wait_send()

    def sent(c, carry):
        main(c, c * N).wait_send()
        return carry

    lax.fori_loop(0, jnp.where(first, CHUNKS, BACK), sent, 0)

    def passed(c, carry):
        for side in (0, 1):
            strip(0, c, 1 + c * N, side).wait_send()
        return carry

    lax.fori_loop(0, jnp.where(first, BACK, CHUNKS), passed, 0)
    for k in (1, 0):
        for way in (0, 1):
            ok = has_dn if way == 0 else has_up

            @pl.when(ok if k else ok & second)
            def _():
                for cp in rows(k, way):
                    cp.wait_send()
    store(0, SHARE_LO, 0).wait()
    store(SHARE_HI, H, 1).wait()
    store(SHARE_LO, SHARE_HI, 2).wait()


def body(latents, conv_weight, conv_bias, norm_gain, norm_shift):
    any_spec = pl.BlockSpec(memory_space=pl.ANY)
    vmem = pl.BlockSpec(memory_space=pltpu.VMEM)
    dma = pltpu.SemaphoreType.DMA
    halo = pltpu.VMEM((4, H + 2, WD, C), BF16)
    ends = pltpu.VMEM((4, H + 2, EDGE, C), BF16)
    return pl.pallas_call(
        kernel,
        out_shape=jax.ShapeDtypeStruct(latents.shape, BF16),
        in_specs=[any_spec, any_spec, vmem, vmem, vmem],
        out_specs=any_spec,
        scratch_shapes=[
            pltpu.VMEM((3, 3, 3 * C, C), BF16), halo, halo, halo, ends, ends,
            pltpu.VMEM((2, ACC_ROWS, WD, C), F32), pltpu.VMEM((2, H, WD, C), BF16),
            pltpu.VMEM((C, 128), F32), pltpu.VMEM((128, C), F32),
            pltpu.VMEM((8, C), F32), pltpu.VMEM((8, 128), F32),
            pltpu.VMEM((8, 8, 128), F32), pltpu.VMEM((16, 8, 128), F32),
            dma((CHUNKS,)), dma((3,)), dma((3,)), dma((CHUNKS,)), dma((CHUNKS,)),
            dma((2, CHUNKS, 2)), dma((2, CHUNKS, 2)), dma((2, 2, 3)), dma((2, 2, 3)),
            dma((7,)), dma((7,)), dma((15,)), dma((15,)),
        ],
        compiler_params=pltpu.CompilerParams(
            collective_id=0, has_side_effects=True, vmem_limit_bytes=56 * 2**20),
        cost_estimate=pl.CostEstimate(flops=20 * 10**9, bytes_accessed=16 * 2**20, transcendentals=10**6),
        name="conv_norm_silu",
    )(
        latents, conv_weight.reshape(3, 3, 3 * C, C), conv_bias.reshape(1, C),
        norm_gain.reshape(1, C), norm_shift.reshape(1, C))


def solution(mesh):
    spec = P("tm", "lat", "lon", None)
    return jax.shard_map(
        body, mesh=mesh, in_specs=(spec, P(), P(), P(), P()), out_specs=spec, check_vma=False)
```

time: 309 us -> 111 us (0.36); the launches traced: 305 us -> 111 us
  blocking collectives: 128 us -> 0 us
  Pallas kernels: 0 us -> 104 us
  waiting for transfers between devices: 48.5 us -> 0 us
  matrix products: 43.1 us -> 0 us
  other arithmetic: 34.1 us -> 0 us
  local copies, waits for them, and re-layouts: 39.7 us -> 6.79 us
  starting transfers between devices: 10.5 us -> 0 us
    psum x2 -> x0, blocking collectives: 128 us -> none  [the longest x1 64.1 us: body(): group_mean = lax.psum(local_sum, ('tm', 'lat', 'lon')) / cell_count]
    pallas_call x0 -> x1, Pallas kernels: none -> 104 us  [body(): pl.pallas_call(kernel, out_shape=jax.ShapeDtypeStruct(latents.shape, BF16...]
    ppermute x5 -> x0, waiting for transfers between devices: 48.5 us -> none  [the longest x1 46.9 us: from_behind(): return lax.ppermute(block, axis, route)]
    dot_general x9 -> x0, matrix products: 43.1 us -> none  [body(): jnp.dot(stacked, kernel, preferred_element_type=jnp.float32)]
    slice x5 -> x0, local copies, waits for them, and re-layouts: 30.1 us -> none  [the longest x1 26.5 us: body(): row_band[:, :, col_k:col_k + lon_cells]]
    concatenate x10 -> x0, other arithmetic: 26.2 us -> none  [the longest x8 16.3 us: body(): jnp.concatenate([row_band[:, :, col_k:col_k + lon_cells] for col_k in ran...]
    ppermute x5 -> x0, starting transfers between devices: 10.5 us -> none  [the longest x2 5.53 us: with_halo(): after = lax.ppermute(initial, axis, down)]
    convert_element_type x1 -> x0, other arithmetic: 4.65 us -> none  [body(): decoded = jax.nn.silu(normed).astype(jnp.bfloat16)]
  transfers between devices with their start and end apart: 5 -> 0, of which waited for: 2 -> 0; matrix products, arithmetic and copies ran while one was open for 3% -> 0% of each run, Pallas kernels for 0% -> 0%
where the time goes in v1:
time: 111 us
  Pallas kernels  104 us (94%)
  local copies, waits for them, and re-layouts  6.79 us (6%)
    pallas_call x1, Pallas kernels, body(): pl.pallas_call(kernel, out_shape=jax.ShapeDtypeStruct(latents.shape, BF16...  104 us
    unnamed x1, local copies, waits for them, and re-layouts  3.02 us

profile of v1, /device:TPU:16, one launch (start us, length us, event | category | flops | bytes accessed | tf_op | source)
XLA Modules:
  0.0 110.6 jit_solution(15636127321767838650)
XLA Ops:
  0.0 1.2 %reshape.13.bias_ref = f32[1,384]{1,0:T(1,128)} reshape(f32[384]{0:T(512)} %param.7) | data formatting | bytes 3072 | tf_op jit(solution)/shard_map/reshape | solution.py:428
  1.2 1.3 %reshape.14.gain_ref = f32[1,384]{1,0:T(1,128)} reshape(f32[384]{0:T(512)} %param.8) | data formatting | bytes 3072 | tf_op jit(solution)/shard_map/reshape | solution.py:429
  2.5 1.3 %reshape.15.shift_ref = f32[1,384]{1,0:T(1,128)} reshape(f32[384]{0:T(512)} %param.9) | data formatting | bytes 3072 | tf_op jit(solution)/shard_map/reshape | solution.py:429
  3.8 103.8 %conv_norm_silu.1 = bf16[2,40,32,384]{3,2,1,0:T(8,128)(2,1)} custom-call(bf16[2,40,32,384]{3,2,1,0:T(8,128)(2,1)} %x_ref.1, bf16[3,3,1152,384]{3,2,1,0:T(8,128)(2,1)} %bitcast.1, f32[1,384]{1,0:T(1,128)} %reshape.13.bias_ref, f32[1,384]{1,0:T(1,128)} %reshape.14.gain_ref, f32[1,384]{1,0:T(1,128)} %reshape.15.shift_ref), custom_call_target="tpu_custom_call" | custom-call | flops 20000000000 | bytes 16777216 | tf_op jit(solution)/shard_map/conv_norm_silu/pallas_call | solution.py:408
  107.6 3.0 %copy.7 = bf16[2,40,32,384]{3,2,1,0:T(8,128)(2,1)} copy(bf16[2,40,32,384]{3,2,1,0:T(8,128)(2,1)} %conv_norm_silu.1) | data formatting | bytes 3932160

commit v2 on v1

--- a/solution.py
+++ b/solution.py
@@ -17,13 +17,14 @@
 H, WD = 40, 32
 N = 4
 CHUNKS = H // N
-EDGE = 16
 
 SHARE_LO, SHARE_HI = 15, 29
 BACK = (SHARE_HI - SHARE_LO + 2) // N
 BACK_ROW = SHARE_LO - 1
 OFF = 30
 ACC_ROWS = 62
+LAST = 20
+SKEW = BACK_ROW % N
 
 
 def chunk_row(c):
@@ -33,9 +34,9 @@
 
 
 def kernel(
-    x_ref, w_ref, bias_ref, gain_ref, shift_ref, o_ref,
-    wt, xm, xl, xr, lh, rh, acc, out, g_in, g_out, aff, stat, r1, r2,
-    loc_sem, w_sem, out_sem, main_s, main_r, strip_s, strip_r, row_s, row_r, r1_s, r1_r, r2_s, r2_r,
+    x_ref, w_ref, bias_in, gain_in, shift_in, o_ref,
+    bias_ref, gain_ref, shift_ref,    wt, xm, xl, xr, cs, ch, cc, acc, g_in, g_out, aff, stat, r1, r2,
+    loc_sem, w_sem, par_sem, main_s, main_r, strip_s, strip_r, own_s, own_r, end_s, end_r, back_s, back_r, row_s, row_r, r1_s, r1_r, r2_s, r2_r,
 ):
     tm, lat, lon = (lax.axis_index(a) for a in ("tm", "lat", "lon"))
     left, right = (lon + 15) % 16, (lon + 1) % 16
@@ -51,7 +52,8 @@
     corners = [(tm, (lat + b) % 4, l) for b in (0, 1, 3) for l in (left, right)]
 
     barrier = pltpu.get_barrier_semaphore()
-    peers = far + near + corners
+    across = [(1 - tm, lat, right), (1 - tm, lat, left)]
+    peers = far + near + corners + across
     for peer in peers:
         pl.semaphore_signal(barrier, inc=1, device_id=peer, device_id_type=MESH)
 
@@ -62,12 +64,15 @@
     def load_w(a):
         return pltpu.make_async_copy(w_ref.at[a], wt.at[a], w_sem.at[a])
 
-    load_x(0).start()
-    load_w(2).start()
-    load_w(1).start()
-    for c in range(1, CHUNKS):
+    params = [
+        pltpu.make_async_copy(src, dst, par_sem.at[i])
+        for i, (src, dst) in enumerate(((bias_in, bias_ref), (gain_in, gain_ref), (shift_in, shift_ref)))]
+    for cp in params:
+        cp.start()
+    for c in range(CHUNKS):
         load_x(c).start()
-    load_w(0).start()
+    for a in (2, 1, 0):
+        load_w(a).start()
 
     row_i = lax.broadcasted_iota(jnp.int32, (C, 128), 0)
     lane_i = lax.broadcasted_iota(jnp.int32, (C, 128), 1)
@@ -78,6 +83,19 @@
     delta = lane_i - PER * row_i
     g_out[...] = jnp.where((delta >= 0) & (delta < PER), 1.0, 0.0)
 
+    def columns(k, c, p):
+        ends = [xm[2 * k + f, p + r].astype(F32) for f in range(2) for r in range(N)]
+        for i, v in enumerate(ends):
+            cs[k, c, 0, i : i + 1] = v[WD - 1:]
+            cs[k, c, 1, i : i + 1] = v[:1]
+
+    def own_columns(c, carry):
+        load_x(c).wait()
+        columns(1, c, 1 + c * N)
+        return carry
+
+    lax.fori_loop(0, CHUNKS, own_columns, 0)
+
     pl.semaphore_wait(barrier, len(peers))
 
     def remote(src, dst, s, r, dev):
@@ -89,25 +107,33 @@
             x_ref.at[:, pl.ds(row, N)], xm.at[pl.ds(0, 2), pl.ds(row + 1, N)],
             main_s.at[c], main_r.at[c], partner)
 
-    def strip(k, c, p, side):
-        cols = pl.ds(WD - EDGE, EDGE) if side == 0 else pl.ds(0, EDGE)
-        src = (
-            x_ref.at[:, pl.ds(p - 1, N), cols] if k else xm.at[pl.ds(0, 2), pl.ds(p, N), cols])
-        dst = (lh, rh)[side].at[pl.ds(2 * k, 2), pl.ds(p, N)]
-        return remote(src, dst, strip_s.at[k, c, side], strip_r.at[k, c, side],
+    def strip(c, side):
+        return remote(cs.at[0, c, side], ch.at[0, c, side], strip_s.at[c, side], strip_r.at[c, side],
                       (tm, lat, (right, left)[side]))
+
+    def own_strip(side):
+        return remote(cs.at[1, :, side], ch.at[1, :, side], own_s.at[side], own_r.at[side],
+                      (tm, lat, (right, left)[side]))
+
+    def end_strip(side):
+        return remote(cs.at[1, LAST // N, side], ch.at[0, CHUNKS - 1, side], end_s.at[side], end_r.at[side],
+                      across[side])
+
+    def back_strip():
+        span = pl.ds(BACK_ROW // N, BACK + 1)
+        return remote(ch.at[1, span], ch.at[0, span], back_s.at[0], back_r.at[0], partner)
 
     def rows(k, way):
         p = H if way == 0 else 1
         q = 0 if way == 0 else H + 1
         la = (lat + 1) % 4 if way == 0 else (lat + 3) % 4
         base = x_ref.at[:, pl.ds(p - 1, 1)] if k else xm.at[pl.ds(0, 2), pl.ds(p, 1)]
-        to = (pl.ds(2 * k, 2), pl.ds(q, 1))
+        c = 0 if way == 1 else CHUNKS - 1 if k else 1
         ss, rs = row_s.at[k, way], row_r.at[k, way]
         return [
-            remote(base, xm.at[to], ss.at[0], rs.at[0], (tm, la, lon)),
-            remote(base.at[:, :, pl.ds(WD - EDGE, EDGE)], lh.at[to], ss.at[1], rs.at[1], (tm, la, right)),
-            remote(base.at[:, :, pl.ds(0, EDGE)], rh.at[to], ss.at[2], rs.at[2], (tm, la, left)),
+            remote(base, xm.at[pl.ds(2 * k, 2), pl.ds(q, 1)], ss.at[0], rs.at[0], (tm, la, lon)),
+            remote(cs.at[k, c, 0], cc.at[k, way, 0], ss.at[1], rs.at[1], (tm, la, right)),
+            remote(cs.at[k, c, 1], cc.at[k, way, 1], ss.at[2], rs.at[2], (tm, la, left)),
         ]
 
     def rows_start(k, way):
@@ -116,15 +142,20 @@
             for cp in rows(k, way):
                 cp.start()
 
+    @pl.when(first)
+    def _():
+        for side in (0, 1):
+            end_strip(side).start()
+        main(0, chunk_row(0)).start()
+
+    for side in (0, 1):
+        own_strip(side).start()
     for way in (0, 1):
         rows_start(1, way)
-    for c in range(2):
-        for side in (0, 1):
-            strip(1, c, c * N + 1, side).start()
 
     @pl.when(first)
     def _():
-        for c in range(CHUNKS):
+        for c in range(1, CHUNKS):
             main(c, chunk_row(c)).start()
 
     @pl.when(second)
@@ -132,11 +163,9 @@
         for c in range(BACK):
             main(c, BACK_ROW + c * N).start()
 
-    for c in range(2, CHUNKS):
-        for side in (0, 1):
-            strip(1, c, c * N + 1, side).start()
-
-    bias = jnp.broadcast_to(bias_ref[...][None], (2, WD, C))
+    for cp in params:
+        cp.wait()
+    bias = jnp.broadcast_to(bias_ref[...].reshape(1, 1, C), (2, WD, C))
 
     def fill(r, carry):
         acc[:, r] = bias
@@ -144,12 +173,12 @@
 
     lax.fori_loop(0, ACC_ROWS, fill, 0)
 
-    def shifted(slot, p):
+    def shifted(slot, p, ends, row):
         col = lax.broadcasted_iota(jnp.int32, (WD, C), 0)
         for f in range(2):
             v = xm[slot + f, p].astype(F32)
-            a = lh[slot + f, p].astype(F32)[EDGE - 1:]
-            b = rh[slot + f, p].astype(F32)[:1]
+            i = f * N + row
+            a, b = ends[0, i : i + 1], ends[1, i : i + 1]
             xl[slot + f, p] = jnp.where(col == 0, a, pltpu.roll(v, 1, 0)).astype(BF16)
             xr[slot + f, p] = jnp.where(col == WD - 1, b, pltpu.roll(v, WD - 1, 0)).astype(BF16)
 
@@ -173,7 +202,7 @@
                 for cp in rows(k, way):
                     cp.wait_recv()
                 p = 0 if way == 0 else H + 1
-                shifted(2 * k, p)
+                shifted(2 * k, p, cc.at[k, way], N - 1 if way == 0 else 0)
                 planes(2 * k, p, 1, k == 1, 0, (0,) if way == 0 else (2,))
 
     def other_p(c):
@@ -182,8 +211,12 @@
     def arrive(c):
         p = other_p(c)
         main(c, p - 1).wait_recv()
-        for side in (0, 1):
-            strip(0, c, p, side).start()
+
+        @pl.when(second & (c < CHUNKS - 1))
+        def _():
+            columns(0, c, p)
+            for side in (0, 1):
+                strip(c, side).start()
 
         @pl.when(second & (c == 0))
         def _():
@@ -195,6 +228,13 @@
 
     load_w(2).wait()
     load_w(1).wait()
+
+    for side in (0, 1):
+        own_strip(side).wait_recv()
+
+    @pl.when(second)
+    def _():
+        back_strip().start()
 
     def own_step(i, carry):
         mine = i < CHUNKS
@@ -202,23 +242,24 @@
         slot = jnp.where(mine, 2, 0)
         p = jnp.where(mine, 1 + i * N, BACK_ROW + 1 + j * N)
 
+        @pl.when(first & (i >= CHUNKS - 1) & (i < CHUNKS - 1 + BACK))
+        def _():
+            arrive(i - (CHUNKS - 1))
+
+        @pl.when(i == CHUNKS)
+        def _():
+            back_strip().wait_recv()
+
         @pl.when(mine)
         def _():
-            load_x(i).wait()
-            for side in (0, 1):
-                strip(1, i, p, side).wait_recv()
-
-        @pl.when(first & (i >= CHUNKS - 1) & (i < CHUNKS - 1 + BACK))
-        def _():
-            arrive(i - (CHUNKS - 1))
+            for r in range(N):
+                shifted(2, p + r, ch.at[1, i], r)
 
         @pl.when(i >= CHUNKS)
         def _():
-            for side in (0, 1):
-                strip(0, j, p, side).wait_recv()
-
-        for r in range(N):
-            shifted(slot, p + r)
+            for r in range(N):
+                shifted(0, p + r, ch.at[0, BACK_ROW // N + j + (SKEW + r) // N], (SKEW + r) % N)
+
         planes(slot, p, N, True, jnp.where(mine, 0, OFF))
         return carry
 
@@ -284,23 +325,19 @@
         inv = lax.rsqrt(m2 / total + 1e-6)
         both = channel(pack(jnp.broadcast_to(mean, (8, 128)), jnp.broadcast_to(inv, (8, 128))))
         aff[0:1] = both[0:1]
-        aff[1:2] = both[1:2] * gain_ref[...]
+        aff[1:2] = both[1:2] * gain_ref[...].reshape(1, C)
 
     def finish(lo, hi):
-        mean, scale, shift = aff[0:1], aff[1:2], shift_ref[...]
+        mean, scale, shift = aff[0:1], aff[1:2], shift_ref[...].reshape(1, C)
 
         def step(r, carry):
             v = acc[:, r + 1].reshape(2 * WD, C)
             v = (v - mean) * scale + shift
             v = v / (1.0 + jnp.exp(-v))
-            out[:, r] = v.astype(BF16).reshape(2, WD, C)
+            o_ref[:, r] = v.astype(BF16).reshape(2, WD, C)
             return carry
 
         lax.fori_loop(lo, hi, step, 0)
-
-    def store(lo, hi, i):
-        return pltpu.make_async_copy(
-            out.at[:, pl.ds(lo, hi - lo)], o_ref.at[:, pl.ds(lo, hi - lo)], out_sem.at[i])
 
     @pl.when(second)
     def _():
@@ -318,10 +355,18 @@
 
         @pl.when(second)
         def _():
-            for side in (0, 1):
-                strip(0, s - 1, p, side).wait_recv()
+            @pl.when(s < CHUNKS)
+            def _():
+                for side in (0, 1):
+                    strip(s - 1, side).wait_recv()
+
+            @pl.when(s == CHUNKS)
+            def _():
+                for side in (0, 1):
+                    end_strip(side).wait_recv()
+
             for r in range(N):
-                shifted(0, p + r)
+                shifted(0, p + r, ch.at[0, s - 1], r)
 
         planes(slot, p, N, False, jnp.where(first, OFF, 0))
 
@@ -346,8 +391,6 @@
             stats_end()
             finish(0, SHARE_LO)
             finish(SHARE_HI, H)
-            store(0, SHARE_LO, 0).start()
-            store(SHARE_HI, H, 1).start()
 
         return carry
 
@@ -360,19 +403,15 @@
         stats_end()
         finish(0, SHARE_LO)
         finish(SHARE_HI, H)
-        store(0, SHARE_LO, 0).start()
-        store(SHARE_HI, H, 1).start()
 
     finish(SHARE_LO, SHARE_HI)
-    store(SHARE_LO, SHARE_HI, 2).start()
 
     for i in range(7):
         r1_copy(i).wait_send()
     for i in range(15):
         r2_copy(i).wait_send()
-    for c in range(CHUNKS):
-        for side in (0, 1):
-            strip(1, c, c * N + 1, side).wait_send()
+    for side in (0, 1):
+        own_strip(side).wait_send()
 
     def sent(c, carry):
         main(c, c * N).wait_send()
@@ -380,12 +419,18 @@
 
     lax.fori_loop(0, jnp.where(first, CHUNKS, BACK), sent, 0)
 
-    def passed(c, carry):
+    @pl.when(first)
+    def _():
         for side in (0, 1):
-            strip(0, c, 1 + c * N, side).wait_send()
-        return carry
-
-    lax.fori_loop(0, jnp.where(first, BACK, CHUNKS), passed, 0)
+            end_strip(side).wait_send()
+
+    @pl.when(second)
+    def _():
+        back_strip().wait_send()
+        for c in range(CHUNKS - 1):
+            for side in (0, 1):
+                strip(c, side).wait_send()
+
     for k in (1, 0):
         for way in (0, 1):
             ok = has_dn if way == 0 else has_up
@@ -394,39 +439,38 @@
             def _():
                 for cp in rows(k, way):
                     cp.wait_send()
-    store(0, SHARE_LO, 0).wait()
-    store(SHARE_HI, H, 1).wait()
-    store(SHARE_LO, SHARE_HI, 2).wait()
 
 
 def body(latents, conv_weight, conv_bias, norm_gain, norm_shift):
-    any_spec = pl.BlockSpec(memory_space=pl.ANY)
     vmem = pl.BlockSpec(memory_space=pltpu.VMEM)
+    hbm = pl.BlockSpec(memory_space=pltpu.HBM)
     dma = pltpu.SemaphoreType.DMA
     halo = pltpu.VMEM((4, H + 2, WD, C), BF16)
-    ends = pltpu.VMEM((4, H + 2, EDGE, C), BF16)
+    ends = pltpu.VMEM((2, CHUNKS, 2, 2 * N, C), F32)
     return pl.pallas_call(
         kernel,
-        out_shape=jax.ShapeDtypeStruct(latents.shape, BF16),
-        in_specs=[any_spec, any_spec, vmem, vmem, vmem],
-        out_specs=any_spec,
+        out_shape=pltpu.VMEM(latents.shape, BF16),
+        in_specs=[hbm] * 5,
+        out_specs=vmem,
         scratch_shapes=[
-            pltpu.VMEM((3, 3, 3 * C, C), BF16), halo, halo, halo, ends, ends,
-            pltpu.VMEM((2, ACC_ROWS, WD, C), F32), pltpu.VMEM((2, H, WD, C), BF16),
+            pltpu.VMEM((C,), F32), pltpu.VMEM((C,), F32), pltpu.VMEM((C,), F32),
+            pltpu.VMEM((3, 3, 3 * C, C), BF16), halo, halo, halo, ends, ends, pltpu.VMEM((2, 2, 2, 2 * N, C), F32),
+            pltpu.VMEM((2, ACC_ROWS, WD, C), F32),
             pltpu.VMEM((C, 128), F32), pltpu.VMEM((128, C), F32),
             pltpu.VMEM((8, C), F32), pltpu.VMEM((8, 128), F32),
             pltpu.VMEM((8, 8, 128), F32), pltpu.VMEM((16, 8, 128), F32),
             dma((CHUNKS,)), dma((3,)), dma((3,)), dma((CHUNKS,)), dma((CHUNKS,)),
-            dma((2, CHUNKS, 2)), dma((2, CHUNKS, 2)), dma((2, 2, 3)), dma((2, 2, 3)),
+            dma((CHUNKS, 2)), dma((CHUNKS, 2)), dma((2,)), dma((2,)), dma((2,)), dma((2,)), dma((1,)), dma((1,)),
+            dma((2, 2, 3)), dma((2, 2, 3)),
             dma((7,)), dma((7,)), dma((15,)), dma((15,)),
         ],
         compiler_params=pltpu.CompilerParams(
-            collective_id=0, has_side_effects=True, vmem_limit_bytes=56 * 2**20),
+            collective_id=0, has_side_effects=True, vmem_limit_bytes=48 * 2**20),
         cost_estimate=pl.CostEstimate(flops=20 * 10**9, bytes_accessed=16 * 2**20, transcendentals=10**6),
         name="conv_norm_silu",
     )(
-        latents, conv_weight.reshape(3, 3, 3 * C, C), conv_bias.reshape(1, C),
-        norm_gain.reshape(1, C), norm_shift.reshape(1, C))
+        *(pltpu.with_memory_space_constraint(v, pltpu.HBM) for v in (
+            latents, conv_weight.reshape(3, 3, 3 * C, C), conv_bias, norm_gain, norm_shift)))
 
 
 def solution(mesh):

time: 111 us -> 70.8 us (0.64)
  Pallas kernels: 104 us -> 68.8 us
  local copies, waits for them, and re-layouts: 6.79 us -> 1.27 us
    pallas_call x1, Pallas kernels: 104 us -> 68.8 us  [body(): pl.pallas_call(kernel, out_shape=pltpu.VMEM(latents.shape, BF16), in_spec...]
    reshape x3 -> x0, local copies, waits for them, and re-layouts: 3.77 us -> none  [the longest x1 1.27 us: body(): norm_gain.reshape(1, C)]
    unnamed x1, local copies, waits for them, and re-layouts: 3.02 us -> 1.27 us
where the time goes in v2:
time: 70.8 us; the launch traced here: 70.1 us
  Pallas kernels  68.8 us (97%)
  local copies, waits for them, and re-layouts  1.27 us (2%)
    pallas_call x1, Pallas kernels, body(): pl.pallas_call(kernel, out_shape=pltpu.VMEM(latents.shape, BF16), in_spec...  68.8 us

profile of v2, /device:TPU:16, one launch (start us, length us, event | category | flops | bytes accessed | tf_op | source)
XLA Modules:
  0.0 70.1 jit_solution(10675796645023816139)
XLA Ops:
  0.0 68.8 %conv_norm_silu.1 = bf16[2,40,32,384]{3,2,1,0:T(8,128)(2,1)S(1)} custom-call(bf16[2,40,32,384]{3,2,1,0:T(8,128)(2,1)} %x_ref.1, bf16[3,3,1152,384]{3,2,1,0:T(8,128)(2,1)} %bitcast.1, f32[384]{0:T(512)} %bias_in.1, f32[384]{0:T(512)} %gain_in.1, f32[384]{0:T(512)} %shift_in.1), custom_call_target="tpu_custom_call" | custom-call | flops 20000000000 | bytes 16777216 | tf_op jit(solution)/shard_map/conv_norm_silu/pallas_call | solution.py:450
  68.8 1.3 %copy.7 = bf16[2,40,32,384]{3,2,1,0:T(8,128)(2,1)} copy(bf16[2,40,32,384]{3,2,1,0:T(8,128)(2,1)S(1)} %conv_norm_silu.1) | data formatting | bytes 3932160

commit v3 on v2

--- a/solution.py
+++ b/solution.py
@@ -23,7 +23,8 @@
 BACK_ROW = SHARE_LO - 1
 OFF = 30
 ACC_ROWS = 62
-LAST = 20
+BLOCK = 8
+EARLY = 3
 SKEW = BACK_ROW % N
 
 
@@ -35,8 +36,8 @@
 
 def kernel(
     x_ref, w_ref, bias_in, gain_in, shift_in, o_ref,
-    bias_ref, gain_ref, shift_ref,    wt, xm, xl, xr, cs, ch, cc, acc, g_in, g_out, aff, stat, r1, r2,
-    loc_sem, w_sem, par_sem, main_s, main_r, strip_s, strip_r, own_s, own_r, end_s, end_r, back_s, back_r, row_s, row_r, r1_s, r1_r, r2_s, r2_r,
+    bias_ref, gain_ref, shift_ref,    wt, xm, xl, xr, cs, ch, cc, pk, pr, acc, g_in, g_out, aff, stat, r1, r2,
+    loc_sem, w_sem, par_sem, main_s, main_r, own_s, own_r, pack_s, pack_r, back_s, back_r, row_s, row_r, r1_s, r1_r, r2_s, r2_r,
 ):
     tm, lat, lon = (lax.axis_index(a) for a in ("tm", "lat", "lon"))
     left, right = (lon + 15) % 16, (lon + 1) % 16
@@ -52,8 +53,7 @@
     corners = [(tm, (lat + b) % 4, l) for b in (0, 1, 3) for l in (left, right)]
 
     barrier = pltpu.get_barrier_semaphore()
-    across = [(1 - tm, lat, right), (1 - tm, lat, left)]
-    peers = far + near + corners + across
+    peers = far + near + corners
     for peer in peers:
         pl.semaphore_signal(barrier, inc=1, device_id=peer, device_id_type=MESH)
 
@@ -62,7 +62,7 @@
             x_ref.at[:, pl.ds(c * N, N)], xm.at[pl.ds(2, 2), pl.ds(c * N + 1, N)], loc_sem.at[c])
 
     def load_w(a):
-        return pltpu.make_async_copy(w_ref.at[a], wt.at[a], w_sem.at[a])
+        return pltpu.make_async_copy(w_ref.at[a], wt.at[:, :, pl.ds((2 - a) * C, C)], w_sem.at[a])
 
     params = [
         pltpu.make_async_copy(src, dst, par_sem.at[i])
@@ -107,17 +107,12 @@
             x_ref.at[:, pl.ds(row, N)], xm.at[pl.ds(0, 2), pl.ds(row + 1, N)],
             main_s.at[c], main_r.at[c], partner)
 
-    def strip(c, side):
-        return remote(cs.at[0, c, side], ch.at[0, c, side], strip_s.at[c, side], strip_r.at[c, side],
-                      (tm, lat, (right, left)[side]))
-
     def own_strip(side):
         return remote(cs.at[1, :, side], ch.at[1, :, side], own_s.at[side], own_r.at[side],
                       (tm, lat, (right, left)[side]))
 
-    def end_strip(side):
-        return remote(cs.at[1, LAST // N, side], ch.at[0, CHUNKS - 1, side], end_s.at[side], end_r.at[side],
-                      across[side])
+    def pack_strip():
+        return remote(pk, pr, pack_s.at[0], pack_r.at[0], partner)
 
     def back_strip():
         span = pl.ds(BACK_ROW // N, BACK + 1)
@@ -142,36 +137,24 @@
             for cp in rows(k, way):
                 cp.start()
 
-    @pl.when(first)
-    def _():
-        for side in (0, 1):
-            end_strip(side).start()
-        main(0, chunk_row(0)).start()
-
     for side in (0, 1):
         own_strip(side).start()
+
+    @pl.when(first)
+    def _():
+        for c in range(EARLY):
+            main(c, chunk_row(c)).start()
+
     for way in (0, 1):
         rows_start(1, way)
 
-    @pl.when(first)
-    def _():
-        for c in range(1, CHUNKS):
-            main(c, chunk_row(c)).start()
-
     @pl.when(second)
     def _():
-        for c in range(BACK):
+        for c in range(2):
             main(c, BACK_ROW + c * N).start()
 
     for cp in params:
         cp.wait()
-    bias = jnp.broadcast_to(bias_ref[...].reshape(1, 1, C), (2, WD, C))
-
-    def fill(r, carry):
-        acc[:, r] = bias
-        return carry
-
-    lax.fori_loop(0, ACC_ROWS, fill, 0)
 
     def shifted(slot, p, ends, row):
         col = lax.broadcasted_iota(jnp.int32, (WD, C), 0)
@@ -182,89 +165,98 @@
             xl[slot + f, p] = jnp.where(col == 0, a, pltpu.roll(v, 1, 0)).astype(BF16)
             xr[slot + f, p] = jnp.where(col == WD - 1, b, pltpu.roll(v, WD - 1, 0)).astype(BF16)
 
-    def planes(slot, p, n, own, off, taps=(0, 1, 2)):
-        m = n * WD
-        both = jnp.concatenate(
-            [v[pl.ds(slot, 2), pl.ds(p, n)].reshape(2 * m, C) for v in (xl, xm, xr)], axis=1)
-        one = both[:m] if own else both[m:]
-        same, target = (2, 1) if own else (0, 0)
-        for b in taps:
+    def taps(slot, p, n):
+        return [v[slot, pl.ds(p, n)].reshape(n * WD, C) for v in (xl, xm, xr)]
+
+    def own_planes(slot, h, off):
+        ahead = [jnp.concatenate([v for b in range(3) for v in taps(slot + f, h + b, BLOCK)], axis=1) for f in range(2)]
+        y = jnp.dot(ahead[0], wt[:, :, : 2 * C].reshape(9 * C, 2 * C), preferred_element_type=F32)
+        z = jnp.dot(ahead[1], wt[:, :, :C].reshape(9 * C, C), preferred_element_type=F32)
+        bias = bias_ref[...].reshape(1, C)
+        rr = pl.ds(h + 1 + off, BLOCK)
+        acc[0, rr] = (y[:, :C] + bias).reshape(BLOCK, WD, C)
+        acc[1, rr] = (y[:, C:] + z + bias).reshape(BLOCK, WD, C)
+
+    def prev_planes(slot, p, n, off, rows_b=(0, 1, 2)):
+        older = jnp.concatenate(taps(slot, p, n), axis=1)
+        newer = jnp.concatenate(taps(slot + 1, p, n), axis=1)
+        for b in rows_b:
             rr = pl.ds(p + 1 - b + off, n)
-            y = jnp.dot(both, wt[same, b], preferred_element_type=F32)
-            acc[:, rr] += y.reshape(2, n, WD, C)
-            y = jnp.dot(one, wt[1, b], preferred_element_type=F32)
-            acc[target, rr] += y.reshape(n, WD, C)
-
-    def edges(k):
+            z = jnp.dot(older, wt[b, :, 2 * C :], preferred_element_type=F32)
+            y = jnp.dot(newer, wt[b, :, C:], preferred_element_type=F32)
+            acc[0, rr] += (y[:, :C] + z).reshape(n, WD, C)
+            acc[1, rr] += y[:, C:].reshape(n, WD, C)
+
+    def edge_rows(k):
         for way in (0, 1):
-            @pl.when(has_up if way == 0 else has_dn)
+            ok = has_up if way == 0 else has_dn
+            p = 0 if way == 0 else H + 1
+
+            @pl.when(ok)
             def _():
                 for cp in rows(k, way):
                     cp.wait_recv()
-                p = 0 if way == 0 else H + 1
                 shifted(2 * k, p, cc.at[k, way], N - 1 if way == 0 else 0)
-                planes(2 * k, p, 1, k == 1, 0, (0,) if way == 0 else (2,))
+                if k == 0:
+                    prev_planes(0, p, 1, 0, (0,) if way == 0 else (2,))
+
+            if k:
+                @pl.when(jnp.logical_not(ok))
+                def _():
+                    for v in (xl, xm, xr):
+                        v[pl.ds(2, 2), pl.ds(p, 1)] = jnp.zeros((2, 1, WD, C), BF16)
 
     def other_p(c):
         return jnp.where(first, BACK_ROW + 1 + c * N, chunk_row(c) + 1)
 
-    def arrive(c):
-        p = other_p(c)
-        main(c, p - 1).wait_recv()
-
-        @pl.when(second & (c < CHUNKS - 1))
-        def _():
-            columns(0, c, p)
-            for side in (0, 1):
-                strip(c, side).start()
-
-        @pl.when(second & (c == 0))
-        def _():
-            rows_start(0, 1)
-
-        @pl.when(second & (c == 1))
-        def _():
-            rows_start(0, 0)
-
+    for side in (0, 1):
+        own_strip(side).wait_recv()
+
+    @pl.when(second)
+    def _():
+        back_strip().start()
+        for c in range(2, BACK):
+            main(c, BACK_ROW + c * N).start()
+
+    @pl.when(first)
+    def _():
+        for side in (0, 1):
+            for t in range(CHUNKS // 2):
+                pk[side, t] = jnp.concatenate([ch[1, 2 * t, side], ch[1, 2 * t + 1, side]], axis=0).astype(BF16)
+        pack_strip().start()
+        for c in range(EARLY, CHUNKS):
+            main(c, chunk_row(c)).start()
+
+    def own_shift(q):
+        for r in range(N):
+            shifted(2, 1 + q * N + r, ch.at[1, q], r)
+
+    for q in range(3):
+        own_shift(q)
+    edge_rows(1)
     load_w(2).wait()
     load_w(1).wait()
-
-    for side in (0, 1):
-        own_strip(side).wait_recv()
-
-    @pl.when(second)
-    def _():
-        back_strip().start()
+    blocks = H // BLOCK
 
     def own_step(i, carry):
-        mine = i < CHUNKS
-        j = jnp.maximum(i - CHUNKS, 0)
-        slot = jnp.where(mine, 2, 0)
-        p = jnp.where(mine, 1 + i * N, BACK_ROW + 1 + j * N)
-
-        @pl.when(first & (i >= CHUNKS - 1) & (i < CHUNKS - 1 + BACK))
-        def _():
-            arrive(i - (CHUNKS - 1))
-
-        @pl.when(i == CHUNKS)
+        mine = i < blocks
+
+        @pl.when(i == blocks)
         def _():
             back_strip().wait_recv()
-
-        @pl.when(mine)
-        def _():
-            for r in range(N):
-                shifted(2, p + r, ch.at[1, i], r)
-
-        @pl.when(i >= CHUNKS)
-        def _():
-            for r in range(N):
-                shifted(0, p + r, ch.at[0, BACK_ROW // N + j + (SKEW + r) // N], (SKEW + r) % N)
-
-        planes(slot, p, N, True, jnp.where(mine, 0, OFF))
+            for j in range(BACK):
+                p = BACK_ROW + 1 + j * N
+                main(j, p - 1).wait_recv()
+                for r in range(N):
+                    shifted(0, p + r, ch.at[0, BACK_ROW // N + j + (SKEW + r) // N], (SKEW + r) % N)
+
+        own_planes(
+            jnp.where(mine, 2, 0), jnp.where(mine, i * BLOCK, BACK_ROW + (i - blocks) * BLOCK), jnp.where(mine, 0, OFF))
+        for k in (3, 4):
+            own_shift(jnp.minimum(2 * i + k, CHUNKS - 1))
         return carry
 
-    lax.fori_loop(0, jnp.where(first, CHUNKS + BACK, CHUNKS), own_step, 0)
-    edges(1)
+    lax.fori_loop(0, jnp.where(first, blocks + BACK * N // BLOCK, blocks), own_step, 0)
     load_w(0).wait()
 
     count = jnp.where(first, 54.0, 26.0) * (2 * WD * PER)
@@ -341,52 +333,54 @@
 
     @pl.when(second)
     def _():
-        arrive(0)
-
-    last_whole = 7
-
-    def prev_step(s, carry):
-        @pl.when(second & (s < last_whole))
-        def _():
-            arrive(s)
-
-        p = other_p(s - 1)
+        pack_strip().wait_recv()
+        for side in (0, 1):
+            for t in range(CHUNKS // 2):
+                v = pr[side, t].astype(F32)
+                ch[0, 2 * t, side] = v[: 2 * N]
+                ch[0, 2 * t + 1, side] = v[2 * N :]
+
+    whole = 6
+
+    def prev_step(c, carry):
+        row = jnp.where(first, BACK_ROW + c * N, chunk_row(c))
+        p = row + 1
         slot = jnp.where(first, 2, 0)
 
         @pl.when(second)
         def _():
-            @pl.when(s < CHUNKS)
-            def _():
-                for side in (0, 1):
-                    strip(s - 1, side).wait_recv()
-
-            @pl.when(s == CHUNKS)
-            def _():
-                for side in (0, 1):
-                    end_strip(side).wait_recv()
+            main(c, row).wait_recv()
+
+            @pl.when(c < 2)
+            def _():
+                columns(0, c, p)
+
+            @pl.when(c == 0)
+            def _():
+                rows_start(0, 1)
+
+            @pl.when(c == 1)
+            def _():
+                rows_start(0, 0)
+
+            @pl.when(c == whole - 1)
+            def _():
+                edge_rows(0)
 
             for r in range(N):
-                shifted(0, p + r, ch.at[0, s - 1], r)
-
-        planes(slot, p, N, False, jnp.where(first, OFF, 0))
-
-        @pl.when(second & (s == 4))
-        def _():
-            edges(0)
-
-        @pl.when(second & (s == last_whole))
+                shifted(0, p + r, ch.at[0, row // N], r)
+
+        prev_planes(slot, p, N, jnp.where(first, OFF, 0))
+
+        @pl.when(second & (c == whole))
         def _():
             stats_begin()
 
-        @pl.when(second & (s == last_whole + 1))
+        @pl.when(second & (c == whole + 1))
         def _():
             stats_middle()
 
-        @pl.when(second & (s >= last_whole) & (s < CHUNKS))
-        def _():
-            arrive(s)
-
-        @pl.when(second & (s == last_whole + 2))
+        @pl.when(second & (c == whole + 2))
         def _():
             stats_end()
             finish(0, SHARE_LO)
@@ -394,7 +388,7 @@
 
         return carry
 
-    lax.fori_loop(1, jnp.where(first, BACK, CHUNKS) + 1, prev_step, 0)
+    lax.fori_loop(0, jnp.where(first, BACK, CHUNKS), prev_step, 0)
 
     @pl.when(first)
     def _():
@@ -421,15 +415,11 @@
 
     @pl.when(first)
     def _():
-        for side in (0, 1):
-            end_strip(side).wait_send()
+        pack_strip().wait_send()
 
     @pl.when(second)
     def _():
         back_strip().wait_send()
-        for c in range(CHUNKS - 1):
-            for side in (0, 1):
-                strip(c, side).wait_send()
 
     for k in (1, 0):
         for way in (0, 1):
@@ -447,6 +437,7 @@
     dma = pltpu.SemaphoreType.DMA
     halo = pltpu.VMEM((4, H + 2, WD, C), BF16)
     ends = pltpu.VMEM((2, CHUNKS, 2, 2 * N, C), F32)
+    packed = pltpu.VMEM((2, CHUNKS // 2, 4 * N, C), BF16)
     return pl.pallas_call(
         kernel,
         out_shape=pltpu.VMEM(latents.shape, BF16),
@@ -454,13 +445,14 @@
         out_specs=vmem,
         scratch_shapes=[
             pltpu.VMEM((C,), F32), pltpu.VMEM((C,), F32), pltpu.VMEM((C,), F32),
-            pltpu.VMEM((3, 3, 3 * C, C), BF16), halo, halo, halo, ends, ends, pltpu.VMEM((2, 2, 2, 2 * N, C), F32),
+            pltpu.VMEM((3, 3 * C, 3 * C), BF16), halo, halo, halo, ends, ends, pltpu.VMEM((2, 2, 2, 2 * N, C), F32),
+            packed, packed,
             pltpu.VMEM((2, ACC_ROWS, WD, C), F32),
             pltpu.VMEM((C, 128), F32), pltpu.VMEM((128, C), F32),
             pltpu.VMEM((8, C), F32), pltpu.VMEM((8, 128), F32),
             pltpu.VMEM((8, 8, 128), F32), pltpu.VMEM((16, 8, 128), F32),
             dma((CHUNKS,)), dma((3,)), dma((3,)), dma((CHUNKS,)), dma((CHUNKS,)),
-            dma((CHUNKS, 2)), dma((CHUNKS, 2)), dma((2,)), dma((2,)), dma((2,)), dma((2,)), dma((1,)), dma((1,)),
+            dma((2,)), dma((2,)), dma((1,)), dma((1,)), dma((1,)), dma((1,)),
             dma((2, 2, 3)), dma((2, 2, 3)),
             dma((7,)), dma((7,)), dma((15,)), dma((15,)),
         ],

time: 70.8 us -> 60.4 us (0.85)
  Pallas kernels: 68.8 us -> 58.5 us
    pallas_call x1, Pallas kernels: 68.8 us -> 58.5 us  [body(): pl.pallas_call(kernel, out_shape=pltpu.VMEM(latents.shape, BF16), in_spec...]
where the time goes in v3:
time: 60.4 us; the launch traced here: 59.8 us
  Pallas kernels  58.5 us (97%)
  local copies, waits for them, and re-layouts  1.27 us (2%)
    pallas_call x1, Pallas kernels, body(): pl.pallas_call(kernel, out_shape=pltpu.VMEM(latents.shape, BF16), in_spec...  58.5 us
    unnamed x1, local copies, waits for them, and re-layouts  1.27 us

profile of v3, /device:TPU:16, one launch (start us, length us, event | category | flops | bytes accessed | tf_op | source)
XLA Modules:
  0.0 59.8 jit_solution(8619542178010350303)
XLA Ops:
  0.0 58.5 %conv_norm_silu.1 = bf16[2,40,32,384]{3,2,1,0:T(8,128)(2,1)S(1)} custom-call(bf16[2,40,32,384]{3,2,1,0:T(8,128)(2,1)} %x_ref.1, bf16[3,3,1152,384]{3,2,1,0:T(8,128)(2,1)} %bitcast.1, f32[384]{0:T(512)} %bias_in.1, f32[384]{0:T(512)} %gain_in.1, f32[384]{0:T(512)} %shift_in.1), custom_call_target="tpu_custom_call" | custom-call | flops 20000000000 | bytes 16777216 | tf_op jit(solution)/shard_map/conv_norm_silu/pallas_call | solution.py:441
  58.5 1.3 %copy.7 = bf16[2,40,32,384]{3,2,1,0:T(8,128)(2,1)} copy(bf16[2,40,32,384]{3,2,1,0:T(8,128)(2,1)S(1)} %conv_norm_silu.1) | data formatting | bytes 3932160

commit v4 on v3

v4 whole, which is shorter than its diff:
```python
import functools

import jax
import jax.numpy as jnp
from jax import lax
from jax.experimental import pallas as pl
from jax.experimental.pallas import tpu as pltpu
from jax.sharding import PartitionSpec as P

MESH = pl.DeviceIdType.MESH
F32, BF16 = jnp.float32, jnp.bfloat16
HIGH = lax.Precision.HIGHEST

GROUPS = 32
C = 384
PER = C // GROUPS
H, WD = 40, 32
N = 4
CHUNKS = H // N

SHARE_LO, SHARE_HI = 11, 29
BACK = (SHARE_HI - SHARE_LO + 2) // N
BACK_ROW = SHARE_LO - 1
OFF = 33
ACC_ROWS = 64
BLOCK = 8
SHARE_BLOCK = 10
SHARED = SHARE_HI - SHARE_LO
EARLY = 3
SKEW = BACK_ROW % N
PAIRS = CHUNKS // 2
END_LO, END_HI = 19, 25
PIVOT = 6


def chunk_row(c):
    odd = c % 2
    half = c // 2
    return N * ((1 - odd) * half + odd * (CHUNKS - 1 - half))


def kernel(
    x_ref, w_ref, bias_in, gain_in, shift_in, o_ref,
    bias_ref, gain_ref, shift_ref,    wt, xm, xl, xr, ends, cs, ph, ch, cc, acc, g_in, g_out, aff, stat, r1, r2,
    loc_sem, w_sem, par_sem, main_s, main_r, own_s, own_r, pack_s, pack_r, back_s, back_r, row_s, row_r, r1_s, r1_r, r2_s, r2_r,
):
    tm, lat, lon = (lax.axis_index(a) for a in ("tm", "lat", "lon"))
    left, right = (lon + 15) % 16, (lon + 1) % 16
    z, yl = lon % 8, lon // 8
    first, second = tm == 0, tm == 1
    has_up, has_dn = lat > 0, lat < 3
    partner = (1 - tm, lat, lon)
    near = [(tm, lat, yl * 8 + (z + d) % 8) for d in range(1, 8)]
    far = [
        ((tm + a) % 2, (lat + b) % 4, ((yl + c) % 2) * 8 + z)
        for a in range(2) for b in range(4) for c in range(2)
    ][1:]

    barrier = pltpu.get_barrier_semaphore()
    for peer in far + near:
        pl.semaphore_signal(barrier, inc=1, device_id=peer, device_id_type=MESH)

    @pl.when(z == 7)
    def _():
        pl.semaphore_signal(barrier, inc=1, device_id=(tm, lat, right), device_id_type=MESH)

    @pl.when(z == 0)
    def _():
        pl.semaphore_signal(barrier, inc=1, device_id=(tm, lat, left), device_id_type=MESH)

    def load_x(c):
        return pltpu.make_async_copy(
            x_ref.at[:, pl.ds(c * N, N)], xm.at[pl.ds(2, 2), pl.ds(c * N + 1, N)], loc_sem.at[c])

    def load_w(a):
        return pltpu.make_async_copy(w_ref.at[a], wt.at[:, :, pl.ds((2 - a) * C, C)], w_sem.at[a])

    params = [
        pltpu.make_async_copy(src, dst, par_sem.at[i])
        for i, (src, dst) in enumerate(((bias_in, bias_ref), (gain_in, gain_ref), (shift_in, shift_ref)))]
    for cp in params:
        cp.start()
    for c in range(CHUNKS):
        load_x(c).start()
    for a in (2, 1, 0):
        load_w(a).start()

    row_i = lax.broadcasted_iota(jnp.int32, (C, 128), 0)
    lane_i = lax.broadcasted_iota(jnp.int32, (C, 128), 1)
    delta = row_i - PER * lane_i
    g_in[...] = jnp.where((delta >= 0) & (delta < PER), 1.0, 0.0)
    row_i = lax.broadcasted_iota(jnp.int32, (128, C), 0)
    lane_i = lax.broadcasted_iota(jnp.int32, (128, C), 1)
    delta = lane_i - PER * row_i
    g_out[...] = jnp.where((delta >= 0) & (delta < PER), 1.0, 0.0)

    def own_columns(t, carry):
        for q in range(2):
            load_x(2 * t + q).wait()
            for f in range(2):
                for r in range(N):
                    v = xm[2 + f, (2 * t + q) * N + 1 + r].astype(F32)
                    i = (2 * q + f) * N + r
                    ends[0, i : i + 1] = v[WD - 1:]
                    ends[1, i : i + 1] = v[:1]
        for side in (0, 1):
            cs[side, t] = ends[side].astype(BF16)
        return carry

    lax.fori_loop(0, PAIRS, own_columns, 0)

    pl.semaphore_wait(barrier, len(far + near) + jnp.where((z == 0) | (z == 7), 1, 0))

    def remote(src, dst, s, r, dev):
        return pltpu.make_async_remote_copy(
            src_ref=src, dst_ref=dst, send_sem=s, recv_sem=r, device_id=dev, device_id_type=MESH)

    def main(c, row):
        return remote(
            x_ref.at[:, pl.ds(row, N)], xm.at[pl.ds(0, 2), pl.ds(row + 1, N)],
            main_s.at[c], main_r.at[c], partner)

    def own_strip(side):
        return remote(cs.at[side], ph.at[1, side], own_s.at[side], own_r.at[side], (tm, lat, (right, left)[side]))

    def pack_strip():
        return remote(ph.at[1], ph.at[0], pack_s.at[0], pack_r.at[0], partner)

    def back_strip():
        span = pl.ds(BACK_ROW // (2 * N), (BACK_ROW + BACK * N - 1) // (2 * N) - BACK_ROW // (2 * N) + 1)
        return remote(ph.at[1, :, span], ph.at[0, :, span], back_s.at[0], back_r.at[0], partner)

    def unpack(k, pairs):
        for t in pairs:
            for side in (0, 1):
                v = ph[k, side, t].astype(F32)
                ch[k, 2 * t, side] = v[: 2 * N]
                ch[k, 2 * t + 1, side] = v[2 * N :]

    def rows(k, way, part):
        la = (lat + 1) % 4 if way == 0 else (lat + 3) % 4
        sems = (row_s.at[k, way, part], row_r.at[k, way, part], (tm, la, lon))
        if part:
            return remote(ch.at[k, 0 if way == 1 else CHUNKS - 1], cc.at[k, way], *sems)
        p = H if way == 0 else 1
        q = 0 if way == 0 else H + 1
        base = x_ref.at[:, pl.ds(p - 1, 1)] if k else xm.at[pl.ds(0, 2), pl.ds(p, 1)]
        return remote(base, xm.at[pl.ds(2 * k, 2), pl.ds(q, 1)], *sems)

    def rows_start(k, way, part):
        @pl.when(has_dn if way == 0 else has_up)
        def _():
            rows(k, way, part).start()

    for side in (0, 1):
        own_strip(side).start()

    @pl.when(first)
    def _():
        for c in range(EARLY):
            main(c, chunk_row(c)).start()

    for way in (0, 1):
        rows_start(1, way, 0)

    @pl.when(second)
    def _():
        for c in range(2):
            main(c, BACK_ROW + c * N).start()

    for cp in params:
        cp.wait()

    def shifted(slot, p, ends, row):
        col = lax.broadcasted_iota(jnp.int32, (WD, C), 0)
        for f in range(2):
            v = xm[slot + f, p].astype(F32)
            i = f * N + row
            a, b = ends[0, i : i + 1], ends[1, i : i + 1]
            xl[slot + f, p] = jnp.where(col == 0, a, pltpu.roll(v, 1, 0)).astype(BF16)
            xr[slot + f, p] = jnp.where(col == WD - 1, b, pltpu.roll(v, WD - 1, 0)).astype(BF16)

    def taps(slot, p, n):
        return [v[slot, pl.ds(p, n)].reshape(n * WD, C) for v in (xl, xm, xr)]

    def own_planes(slot, h, n, off, add):
        ahead = [jnp.concatenate([v for b in range(3) for v in taps(slot + f, h + b, n)], axis=1) for f in range(2)]
        y = jnp.dot(ahead[0], wt[:, :, : 2 * C].reshape(9 * C, 2 * C), preferred_element_type=F32)
        z = jnp.dot(ahead[1], wt[:, :, :C].reshape(9 * C, C), preferred_element_type=F32)
        rr = pl.ds(h + 1 + off, n)
        if add:
            acc[0, rr] += y[:, :C].reshape(n, WD, C)
            acc[1, rr] += (y[:, C:] + z).reshape(n, WD, C)
        else:
            bias = bias_ref[...].reshape(1, C)
            acc[0, rr] = (y[:, :C] + bias).reshape(n, WD, C)
            acc[1, rr] = (y[:, C:] + z + bias).reshape(n, WD, C)

    def prev_planes(slot, p, n, off, rows_b=(0, 1, 2)):
        older = jnp.concatenate(taps(slot, p, n), axis=1)
        newer = jnp.concatenate(taps(slot + 1, p, n), axis=1)
        for b in rows_b:
            rr = pl.ds(p + 1 - b + off, n)
            z = jnp.dot(older, wt[b, :, 2 * C :], preferred_element_type=F32)
            y = jnp.dot(newer, wt[b, :, C:], preferred_element_type=F32)
            acc[0, rr] += (y[:, :C] + z).reshape(n, WD, C)
            acc[1, rr] += y[:, C:].reshape(n, WD, C)

    def prev_block(slot, h, n, off):
        ahead = [jnp.concatenate([v for b in range(3) for v in taps(slot + f, h + b, n)], axis=1) for f in range(2)]
        z = jnp.dot(ahead[0], wt[:, :, 2 * C :].reshape(9 * C, C), preferred_element_type=F32)
        y = jnp.dot(ahead[1], wt[:, :, C:].reshape(9 * C, 2 * C), preferred_element_type=F32)
        bias = bias_ref[...].reshape(1, C)
        rr = pl.ds(h + 1 + off, n)
        acc[0, rr] = (y[:, :C] + z + bias).reshape(n, WD, C)
        acc[1, rr] = (y[:, C:] + bias).reshape(n, WD, C)

    def edge_rows(k):
        for way in (0, 1):
            ok = has_up if way == 0 else has_dn
            p = 0 if way == 0 else H + 1

            @pl.when(ok)
            def _():
                for part in (0, 1):
                    rows(k, way, part).wait_recv()
                shifted(2 * k, p, cc.at[k, way], N - 1 if way == 0 else 0)
                if k == 0:
                    prev_planes(0, p, 1, 0, (0,) if way == 0 else (2,))

            if k:
                @pl.when(jnp.logical_not(ok))
                def _():
                    for v in (xl, xm, xr):
                        v[pl.ds(2, 2), pl.ds(p, 1)] = jnp.zeros((2, 1, WD, C), BF16)

    def other_p(c):
        return jnp.where(first, BACK_ROW + 1 + c * N, chunk_row(c) + 1)

    for side in (0, 1):
        own_strip(side).wait_recv()

    @pl.when(second)
    def _():
        back_strip().start()
        for c in range(2, BACK):
            main(c, BACK_ROW + c * N).start()

    @pl.when(first)
    def _():
        pack_strip().start()
        for c in range(EARLY, CHUNKS):
            main(c, chunk_row(c)).start()

    unpack(1, range(PAIRS))
    for way in (0, 1):
        rows_start(1, way, 1)

    def own_shift(q):
        for r in range(N):
            shifted(2, 1 + q * N + r, ch.at[1, q], r)

    for q in range(1, 5):
        own_shift(q)
    load_w(2).wait()
    load_w(1).wait()
    blocks = H // BLOCK

    def own_step(i, carry):
        @pl.when(i == blocks - 2)
        def _():
            edge_rows(1)

        own_planes(2, (i + 1) % blocks * BLOCK, BLOCK, 0, False)
        for k in (5, 6):
            own_shift((2 * i + k) % CHUNKS)
        return carry

    lax.fori_loop(0, blocks, own_step, 0)
    load_w(0).wait()

    count = jnp.where(first, float(H + SHARED), float(H - SHARED)) * (2 * WD * PER)
    other_count = jnp.where(first, float(H - SHARED), float(H + SHARED)) * (2 * WD * PER)
    sub = lax.broadcasted_iota(jnp.int32, (8, 128), 0)

    def pack(mean, m2):
        return jnp.where(sub == 0, mean, jnp.where(sub == 1, m2, 0.0))

    def over_rows():
        pivot = aff[8:16]

        def step(r, sums):
            d = acc[:, r].reshape(2 * WD // 8, 8, C) - pivot
            return sums[0] + d.sum(0), sums[1] + (d * d).sum(0)

        sums = (jnp.zeros((8, C), F32), jnp.zeros((8, C), F32))
        sums = lax.fori_loop(1, jnp.where(first, 1 + H, 1 + SHARE_LO), step, sums)
        sums = lax.fori_loop(
            jnp.where(first, 1 + SHARE_LO + OFF, 1 + SHARE_HI), jnp.where(first, 1 + SHARE_HI + OFF, 1 + H), step, sums)
        return [jnp.broadcast_to(v.sum(0, keepdims=True), (8, C)) for v in sums]

    def group(v):
        return jnp.dot(v, g_in[...], precision=HIGH, preferred_element_type=F32)

    def channel(v):
        return jnp.dot(v, g_out[...], precision=HIGH, preferred_element_type=F32)

    def r1_copy(i):
        return remote(r1.at[0], r1.at[i + 1], r1_s.at[i], r1_r.at[i], near[i])

    def r2_copy(i):
        return remote(r2.at[0], r2.at[i + 1], r2_s.at[i], r2_r.at[i], far[i])

    def stats_pivot():
        v = acc[:, PIVOT].reshape(2 * WD // 8, 8, C).sum(0).sum(0, keepdims=True)
        mean = group(jnp.broadcast_to(v, (8, C))) * (1.0 / (2 * WD * PER))
        stat[...] = mean
        aff[8:16] = channel(mean)

    def stats_begin():
        s1, s2 = over_rows()
        sums = group(jnp.where(lax.broadcasted_iota(jnp.int32, (8, C), 0) == 0, s1, s2))
        shift = sums[0:1] / count
        m2 = jnp.maximum(sums[1:2] - sums[0:1] * shift, 0.0)
        r1[0] = pack(stat[...] + shift, jnp.broadcast_to(m2, (8, 128)))
        for i in range(7):
            r1_copy(i).start()

    def stats_middle():
        for i in range(7):
            r1_copy(i).wait_recv()
        means = [r1[i, 0:1] for i in range(8)]
        mean = sum(means) * 0.125
        m2 = sum(r1[i, 1:2] for i in range(8)) + count * sum((m - mean) * (m - mean) for m in means)
        r2[0] = pack(jnp.broadcast_to(mean, (8, 128)), jnp.broadcast_to(m2, (8, 128)))
        for i in range(15):
            r2_copy(i).start()

    def stats_end():
        for i in range(15):
            r2_copy(i).wait_recv()
        means = [r2[i, 0:1] for i in range(16)]
        mine, other = 8.0 * count, 8.0 * other_count
        total = 8.0 * (mine + other)
        mean = (mine * sum(means[:8]) + other * sum(means[8:])) / total
        m2 = sum(r2[i, 1:2] for i in range(16))
        m2 = m2 + mine * sum((m - mean) * (m - mean) for m in means[:8])
        m2 = m2 + other * sum((m - mean) * (m - mean) for m in means[8:])
        inv = lax.rsqrt(m2 / total + 1e-6)
        both = channel(pack(jnp.broadcast_to(mean, (8, 128)), jnp.broadcast_to(inv, (8, 128))))
        aff[0:1] = both[0:1]
        aff[1:2] = both[1:2] * gain_ref[...].reshape(1, C)

    def finish(lo, hi):
        mean, scale, shift = aff[0:1], aff[1:2], shift_ref[...].reshape(1, C)

        def step(r, carry):
            v = acc[:, r + 1].reshape(2 * WD, C)
            v = (v - mean) * scale + shift
            v = v / (1.0 + jnp.exp(-v))
            o_ref[:, r] = v.astype(BF16).reshape(2, WD, C)
            return carry

        lax.fori_loop(lo, hi, step, 0)

    @pl.when(second)
    def _():
        pack_strip().wait_recv()
        unpack(0, range(PAIRS))
        for way in (0, 1):
            rows_start(0, way, 1)

    whole = 5

    def prev_step(c, carry):
        row = chunk_row(c)
        p = row + 1
        main(c, row).wait_recv()

        @pl.when(c == 0)
        def _():
            rows_start(0, 1, 0)

        @pl.when(c == 1)
        def _():
            rows_start(0, 0, 0)

        @pl.when(c == whole - 1)
        def _():
            edge_rows(0)
            stats_pivot()

        for r in range(N):
            shifted(0, p + r, ch.at[0, row // N], r)
        prev_planes(0, p, N, 0)

        @pl.when(c == whole)
        def _():
            stats_begin()

        @pl.when(c == whole + 1)
        def _():
            stats_middle()

        @pl.when(c == CHUNKS - 2)
        def _():
            stats_end()
            finish(0, END_LO)
            finish(END_HI, H)

        return carry

    @pl.when(second)
    def _():
        lax.fori_loop(0, CHUNKS, prev_step, 0)
        finish(END_LO, END_HI)

    @pl.when(first)
    def _():
        def shared_prev(i, carry):
            prev_block(2, BACK_ROW + i * SHARE_BLOCK, SHARE_BLOCK, OFF)
            return carry

        lax.fori_loop(0, BACK * N // SHARE_BLOCK, shared_prev, 0)
        stats_pivot()
        back_strip().wait_recv()
        unpack(0, range(BACK_ROW // (2 * N), (BACK_ROW + BACK * N - 1) // (2 * N) + 1))
        for j in range(BACK):
            p = BACK_ROW + 1 + j * N
            main(j, p - 1).wait_recv()
            for r in range(N):
                shifted(0, p + r, ch.at[0, BACK_ROW // N + j + (SKEW + r) // N], (SKEW + r) % N)

        def shared_step(i, carry):
            own_planes(0, BACK_ROW + i * SHARE_BLOCK, SHARE_BLOCK, OFF, True)
            return carry

        lax.fori_loop(0, BACK * N // SHARE_BLOCK, shared_step, 0)
        stats_begin()
        stats_middle()
        stats_end()
        finish(0, H)

    for i in range(7):
        r1_copy(i).wait_send()
    for i in range(15):
        r2_copy(i).wait_send()
    for side in (0, 1):
        own_strip(side).wait_send()

    def sent(c, carry):
        main(c, c * N).wait_send()
        return carry

    lax.fori_loop(0, jnp.where(first, CHUNKS, BACK), sent, 0)

    @pl.when(first)
    def _():
        pack_strip().wait_send()

    @pl.when(second)
    def _():
        back_strip().wait_send()

    for k in (1, 0):
        for way in (0, 1):
            ok = has_dn if way == 0 else has_up

            @pl.when(ok if k else ok & second)
            def _():
                for part in (0, 1):
                    rows(k, way, part).wait_send()


def body(latents, conv_weight, conv_bias, norm_gain, norm_shift):
    vmem = pl.BlockSpec(memory_space=pltpu.VMEM)
    hbm = pl.BlockSpec(memory_space=pltpu.HBM)
    dma = pltpu.SemaphoreType.DMA
    halo = pltpu.VMEM((4, H + 2, WD, C), BF16)
    packed = (2, PAIRS, 4 * N, C)
    return pl.pallas_call(
        kernel,
        out_shape=pltpu.VMEM(latents.shape, BF16),
        in_specs=[hbm] * 5,
        out_specs=vmem,
        scratch_shapes=[
            pltpu.VMEM((C,), F32), pltpu.VMEM((C,), F32), pltpu.VMEM((C,), F32),
            pltpu.VMEM((3, 3 * C, 3 * C), BF16), halo, halo, halo,
            pltpu.VMEM((2, 4 * N, C), F32), pltpu.VMEM(packed, BF16), pltpu.VMEM((2,) + packed, BF16),
            pltpu.VMEM((2, CHUNKS, 2, 2 * N, C), F32), pltpu.VMEM((2, 2, 2, 2 * N, C), F32),
            pltpu.VMEM((2, ACC_ROWS, WD, C), F32),
            pltpu.VMEM((C, 128), F32), pltpu.VMEM((128, C), F32),
            pltpu.VMEM((16, C), F32), pltpu.VMEM((8, 128), F32),
            pltpu.VMEM((8, 8, 128), F32), pltpu.VMEM((16, 8, 128), F32),
            dma((CHUNKS,)), dma((3,)), dma((3,)), dma((CHUNKS,)), dma((CHUNKS,)),
            dma((2,)), dma((2,)), dma((1,)), dma((1,)), dma((1,)), dma((1,)),
            dma((2, 2, 2)), dma((2, 2, 2)),
            dma((7,)), dma((7,)), dma((15,)), dma((15,)),
        ],
        compiler_params=pltpu.CompilerParams(
            collective_id=0, has_side_effects=True, vmem_limit_bytes=48 * 2**20),
        cost_estimate=pl.CostEstimate(flops=20 * 10**9, bytes_accessed=16 * 2**20, transcendentals=10**6),
        name="conv_norm_silu",
    )(
        *(pltpu.with_memory_space_constraint(v, pltpu.HBM) for v in (
            latents, conv_weight.reshape(3, 3, 3 * C, C), conv_bias, norm_gain, norm_shift)))


def solution(mesh):
    spec = P("tm", "lat", "lon", None)
    return jax.shard_map(
        body, mesh=mesh, in_specs=(spec, P(), P(), P(), P()), out_specs=spec, check_vma=False)
```

time: 60.4 us -> 58.9 us (0.975)
  Pallas kernels: 58.5 us -> 57.5 us
    pallas_call x1, Pallas kernels: 58.5 us -> 57.5 us  [body(): pl.pallas_call(kernel, out_shape=pltpu.VMEM(latents.shape, BF16), in_spec...]
where the time goes in v4:
time: 58.9 us; the launch traced here: 58.8 us
  Pallas kernels  57.5 us (98%)
  local copies, waits for them, and re-layouts  1.27 us (2%)
    pallas_call x1, Pallas kernels, body(): pl.pallas_call(kernel, out_shape=pltpu.VMEM(latents.shape, BF16), in_spec...  57.5 us
    unnamed x1, local copies, waits for them, and re-layouts  1.27 us

profile of v4, /device:TPU:16, one launch (start us, length us, event | category | flops | bytes accessed | tf_op | source)
XLA Modules:
  0.0 58.8 jit_solution(7458486665308012489)
XLA Ops:
  0.0 57.5 %conv_norm_silu.1 = bf16[2,40,32,384]{3,2,1,0:T(8,128)(2,1)S(1)} custom-call(bf16[2,40,32,384]{3,2,1,0:T(8,128)(2,1)} %x_ref.1, bf16[3,3,1152,384]{3,2,1,0:T(8,128)(2,1)} %bitcast.1, f32[384]{0:T(512)} %bias_in.1, f32[384]{0:T(512)} %gain_in.1, f32[384]{0:T(512)} %shift_in.1), custom_call_target="tpu_custom_call" | custom-call | flops 20000000000 | bytes 16777216 | tf_op jit(solution)/shard_map/conv_norm_silu/pallas_call | solution.py:481
  57.5 1.3 %copy.7 = bf16[2,40,32,384]{3,2,1,0:T(8,128)(2,1)} copy(bf16[2,40,32,384]{3,2,1,0:T(8,128)(2,1)S(1)} %conv_norm_silu.1) | data formatting | bytes 3932160

commit v5 on v4

--- a/solution.py
+++ b/solution.py
@@ -120,6 +120,12 @@
             x_ref.at[:, pl.ds(row, N)], xm.at[pl.ds(0, 2), pl.ds(row + 1, N)],
             main_s.at[c], main_r.at[c], partner)
 
+    def last(half):
+        row = chunk_row(CHUNKS - 1) + half * N // 2
+        return remote(
+            x_ref.at[:, pl.ds(row, N // 2)], xm.at[pl.ds(0, 2), pl.ds(row + 1, N // 2)],
+            main_s.at[CHUNKS - 1 + half], main_r.at[CHUNKS - 1 + half], partner)
+
     def own_strip(side):
         return remote(cs.at[side], ph.at[1, side], own_s.at[side], own_r.at[side], (tm, lat, (right, left)[side]))
 
@@ -249,8 +255,9 @@
     @pl.when(first)
     def _():
         pack_strip().start()
-        for c in range(EARLY, CHUNKS):
+        for c in range(EARLY, CHUNKS - 1):
             main(c, chunk_row(c)).start()
+        last(0).start()
 
     unpack(1, range(PAIRS))
     for way in (0, 1):
@@ -351,10 +358,11 @@
         aff[0:1] = both[0:1]
         aff[1:2] = both[1:2] * gain_ref[...].reshape(1, C)
 
-    def finish(lo, hi):
+    def finish(lo, hi, skip=0):
         mean, scale, shift = aff[0:1], aff[1:2], shift_ref[...].reshape(1, C)
 
-        def step(r, carry):
+        def step(i, carry):
+            r = i + jnp.where(i >= END_LO, skip, 0)
             v = acc[:, r + 1].reshape(2 * WD, C)
             v = (v - mean) * scale + shift
             v = v / (1.0 + jnp.exp(-v))
@@ -370,12 +378,54 @@
         for way in (0, 1):
             rows_start(0, way, 1)
 
+    def drain():
+        for i in range(7):
+            r1_copy(i).wait_send()
+        for i in range(15):
+            r2_copy(i).wait_send()
+        for side in (0, 1):
+            own_strip(side).wait_send()
+
+        def sent(c, carry):
+            main(c, c * N).wait_send()
+            return carry
+
+        lax.fori_loop(0, jnp.where(first, CHUNKS - 1, BACK), sent, 0)
+
+        @pl.when(first)
+        def _():
+            pack_strip().wait_send()
+            for half in (0, 1):
+                last(half).wait_send()
+
+        @pl.when(second)
+        def _():
+            back_strip().wait_send()
+
+        for k in (1, 0):
+            for way in (0, 1):
+                ok = has_dn if way == 0 else has_up
+
+                @pl.when(ok if k else ok & second)
+                def _():
+                    for part in (0, 1):
+                        rows(k, way, part).wait_send()
+
     whole = 5
 
     def prev_step(c, carry):
         row = chunk_row(c)
         p = row + 1
-        main(c, row).wait_recv()
+
+        @pl.when(c < CHUNKS - 1)
+        def _():
+            main(c, row).wait_recv()
+
+        @pl.when(c == CHUNKS - 1)
+        def _():
+            for half in (0, 1):
+                last(half).wait_recv()
+
 
         @pl.when(c == 0)
         def _():
@@ -405,15 +455,19 @@
         @pl.when(c == CHUNKS - 2)
         def _():
             stats_end()
-            finish(0, END_LO)
-            finish(END_HI, H)
+            drain()
+
+        @pl.when(c >= CHUNKS - 2)
+        def _():
+            early = c == CHUNKS - 2
+            gap = END_HI - END_LO
+            finish(jnp.where(early, 0, END_LO), jnp.where(early, H - gap, END_HI), jnp.where(early, gap, 0))
 
         return carry
 
     @pl.when(second)
     def _():
         lax.fori_loop(0, CHUNKS, prev_step, 0)
-        finish(END_LO, END_HI)
 
     @pl.when(first)
     def _():
@@ -438,39 +492,10 @@
         lax.fori_loop(0, BACK * N // SHARE_BLOCK, shared_step, 0)
         stats_begin()
         stats_middle()
+        last(1).start()
         stats_end()
         finish(0, H)
-
-    for i in range(7):
-        r1_copy(i).wait_send()
-    for i in range(15):
-        r2_copy(i).wait_send()
-    for side in (0, 1):
-        own_strip(side).wait_send()
-
-    def sent(c, carry):
-        main(c, c * N).wait_send()
-        return carry
-
-    lax.fori_loop(0, jnp.where(first, CHUNKS, BACK), sent, 0)
-
-    @pl.when(first)
-    def _():
-        pack_strip().wait_send()
-
-    @pl.when(second)
-    def _():
-        back_strip().wait_send()
-
-    for k in (1, 0):
-        for way in (0, 1):
-            ok = has_dn if way == 0 else has_up
-
-            @pl.when(ok if k else ok & second)
-            def _():
-                for part in (0, 1):
-                    rows(k, way, part).wait_send()
-
+        drain()
 
 def body(latents, conv_weight, conv_bias, norm_gain, norm_shift):
     vmem = pl.BlockSpec(memory_space=pltpu.VMEM)
@@ -492,7 +517,7 @@
             pltpu.VMEM((C, 128), F32), pltpu.VMEM((128, C), F32),
             pltpu.VMEM((16, C), F32), pltpu.VMEM((8, 128), F32),
             pltpu.VMEM((8, 8, 128), F32), pltpu.VMEM((16, 8, 128), F32),
-            dma((CHUNKS,)), dma((3,)), dma((3,)), dma((CHUNKS,)), dma((CHUNKS,)),
+            dma((CHUNKS,)), dma((3,)), dma((3,)), dma((CHUNKS + 1,)), dma((CHUNKS + 1,)),
             dma((2,)), dma((2,)), dma((1,)), dma((1,)), dma((1,)), dma((1,)),
             dma((2, 2, 2)), dma((2, 2, 2)),
             dma((7,)), dma((7,)), dma((15,)), dma((15,)),

time: 58.9 us -> 57.9 us (0.983)
  Pallas kernels: 57.5 us -> 56.5 us
    pallas_call x1, Pallas kernels: 57.5 us -> 56.5 us  [body(): pl.pallas_call(kernel, out_shape=pltpu.VMEM(latents.shape, BF16), in_spec...]
where the time goes in v5:
time: 57.9 us; the launch traced here: 57.8 us
  Pallas kernels  56.5 us (98%)
  local copies, waits for them, and re-layouts  1.27 us (2%)
    pallas_call x1, Pallas kernels, body(): pl.pallas_call(kernel, out_shape=pltpu.VMEM(latents.shape, BF16), in_spec...  56.5 us
    unnamed x1, local copies, waits for them, and re-layouts  1.27 us

profile of v5, /device:TPU:16, one launch (start us, length us, event | category | flops | bytes accessed | tf_op | source)
XLA Modules:
  0.0 57.8 jit_solution(6904927279975157549)
XLA Ops:
  0.0 56.5 %conv_norm_silu.1 = bf16[2,40,32,384]{3,2,1,0:T(8,128)(2,1)S(1)} custom-call(bf16[2,40,32,384]{3,2,1,0:T(8,128)(2,1)} %x_ref.1, bf16[3,3,1152,384]{3,2,1,0:T(8,128)(2,1)} %bitcast.1, f32[384]{0:T(512)} %bias_in.1, f32[384]{0:T(512)} %gain_in.1, f32[384]{0:T(512)} %shift_in.1), custom_call_target="tpu_custom_call" | custom-call | flops 20000000000 | bytes 16777216 | tf_op jit(solution)/shard_map/conv_norm_silu/pallas_call | solution.py:506
  56.5 1.3 %copy.7 = bf16[2,40,32,384]{3,2,1,0:T(8,128)(2,1)} copy(bf16[2,40,32,384]{3,2,1,0:T(8,128)(2,1)S(1)} %conv_norm_silu.1) | data formatting | bytes 3932160

commit v6 on v5

--- a/solution.py
+++ b/solution.py
@@ -121,9 +121,10 @@
             main_s.at[c], main_r.at[c], partner)
 
     def last(half):
-        row = chunk_row(CHUNKS - 1) + half * N // 2
+        row = chunk_row(CHUNKS - 1) + half
+        n = N - 1 if half else 1
         return remote(
-            x_ref.at[:, pl.ds(row, N // 2)], xm.at[pl.ds(0, 2), pl.ds(row + 1, N // 2)],
+            x_ref.at[:, pl.ds(row, n)], xm.at[pl.ds(0, 2), pl.ds(row + 1, n)],
             main_s.at[CHUNKS - 1 + half], main_r.at[CHUNKS - 1 + half], partner)
 
     def own_strip(side):
@@ -333,14 +334,14 @@
         for i in range(7):
             r1_copy(i).start()
 
-    def stats_middle():
+    def stats_middle(order):
         for i in range(7):
             r1_copy(i).wait_recv()
         means = [r1[i, 0:1] for i in range(8)]
         mean = sum(means) * 0.125
         m2 = sum(r1[i, 1:2] for i in range(8)) + count * sum((m - mean) * (m - mean) for m in means)
         r2[0] = pack(jnp.broadcast_to(mean, (8, 128)), jnp.broadcast_to(m2, (8, 128)))
-        for i in range(15):
+        for i in order:
             r2_copy(i).start()
 
     def stats_end():
@@ -450,7 +451,7 @@
 
         @pl.when(c == whole + 1)
         def _():
-            stats_middle()
+            stats_middle(range(15))
 
         @pl.when(c == CHUNKS - 2)
         def _():
@@ -491,7 +492,7 @@
 
         lax.fori_loop(0, BACK * N // SHARE_BLOCK, shared_step, 0)
         stats_begin()
-        stats_middle()
+        stats_middle(range(14, -1, -1))
         last(1).start()
         stats_end()
         finish(0, H)

time: 57.9 us -> 57.6 us (level)
  no operation moved by 1% of the time
where the time goes in v6:
time: 57.6 us; the launch traced here: 57.5 us
  Pallas kernels  56.2 us (98%)
  local copies, waits for them, and re-layouts  1.27 us (2%)
    pallas_call x1, Pallas kernels, body(): pl.pallas_call(kernel, out_shape=pltpu.VMEM(latents.shape, BF16), in_spec...  56.2 us
    unnamed x1, local copies, waits for them, and re-layouts  1.27 us

profile of v6, /device:TPU:16, one launch (start us, length us, event | category | flops | bytes accessed | tf_op | source)
XLA Modules:
  0.0 57.5 jit_solution(11399495350590970805)
XLA Ops:
  0.0 56.2 %conv_norm_silu.1 = bf16[2,40,32,384]{3,2,1,0:T(8,128)(2,1)S(1)} custom-call(bf16[2,40,32,384]{3,2,1,0:T(8,128)(2,1)} %x_ref.1, bf16[3,3,1152,384]{3,2,1,0:T(8,128)(2,1)} %bitcast.1, f32[384]{0:T(512)} %bias_in.1, f32[384]{0:T(512)} %gain_in.1, f32[384]{0:T(512)} %shift_in.1), custom_call_target="tpu_custom_call" | custom-call | flops 20000000000 | bytes 16777216 | tf_op jit(solution)/shard_map/conv_norm_silu/pallas_call | solution.py:507
  56.2 1.3 %copy.7 = bf16[2,40,32,384]{3,2,1,0:T(8,128)(2,1)} copy(bf16[2,40,32,384]{3,2,1,0:T(8,128)(2,1)S(1)} %conv_norm_silu.1) | data formatting | bytes 3932160
